TPU v7x, 512 devices: a whole 4x4x16 slice. The times are simulated.
512 devices in a mesh: gx: 32 (over z_lo, x), gy: 16 (over z_hi, y, core).
Axes of the slice: x: 4, y: 4, z: 16 (z_hi: 2, z_lo: 8; z = z_hi * 8 + z_lo), core: 2. Of those that a mesh axis runs over, the one named last changes fastest.
Arguments:
- displacement: float32 [3, 128, 128, 128], P(None, 'gx', 'gy'), may hold values from -0.15 to 0.15
- velocity: float32 [3, 128, 128, 128], P(None, 'gx', 'gy'), may hold values from -4 to 4
- stiffness: float32 [128, 128, 128], P('gx', 'gy'), may hold values from 0.5 to 4
- damage: int32 [6, 128, 128, 128], P(None, 'gx', 'gy'), may hold values from 0 to 2047, as said below
Outputs:
- new_displacement: float32 [3, 128, 128, 128], P(None, 'gx', 'gy')
- new_velocity: float32 [3, 128, 128, 128], P(None, 'gx', 'gy')
Inputs may be any that keep to these rules, and one draw needn't show every extreme that they name: `damage`: bits above bit 10 are zero; in the last word only bits 0 to 5 are used.
All inputs are finite; a program needn't handle non-finite values.
Results may differ from a plain program's by a relative error of at most 0.0001.
Values sent between devices are 32-bit elements; how exact they have to be, the bound alone decides.
No kernel may reach another device: no remote copies, remote signals or barrier semaphores. Data moves between devices by JAX's collectives and lax.ppermute only.
A program may use at most 64 MiB of HBM per device.

v0:
```python
import math

import jax
import jax.numpy as jnp
from jax import lax
from jax.sharding import PartitionSpec as P

STEPS = 2


time_step = 0.02
bond_scale = 100.0


def shifted(block, axis, distance):
    devices = range(lax.axis_size(axis))
    route = [(i - distance, i) for i in devices if i - distance in devices]
    return lax.ppermute(block, axis, route)


def extended(value, sides, width):
    for axis, dim in sides:
        size, length = (lax.axis_size(axis), value.shape[dim])
        up = [(i, (i + 1) % size) for i in range(size - 1)]
        down = [(j, i) for i, j in up]
        last = lax.slice_in_dim(value, length - width, length, axis=dim)
        initial = lax.slice_in_dim(value, 0, width, axis=dim)
        before = lax.ppermute(last, axis, up)
        after = lax.ppermute(initial, axis, down)
        value = jnp.concatenate([before, value, after], axis=dim)
    return value


def bond_offsets():
    table = []
    for step_x in range(0, 4):
        for step_y in range(-3, 4):
            for step_z in range(-3, 4):
                if step_x * step_x + step_y * step_y + step_z * step_z <= 9 and (
                    step_x,
                    step_y,
                    step_z,
                ) > (0, 0, 0):
                    table.append((step_x, step_y, step_z))
    return table


def bond_force(center, neighbour, center_k, neighbour_k, broken, offset):
    length = math.sqrt(offset[0] ** 2 + offset[1] ** 2 + offset[2] ** 2)
    shift_vec = jnp.array(offset, jnp.float32).reshape(3, 1, 1, 1)
    separation = neighbour - center + shift_vec
    distance = jnp.sqrt(jnp.sum(separation * separation, axis=0))
    factor = (
        bond_scale
        * jnp.sqrt(center_k * neighbour_k)
        * (1.0 - broken)
        * (distance - length)
        / (length * distance)
    )
    return factor[None] * separation


def widened_field(displacement, stiffness):
    joined = jnp.concatenate([displacement, stiffness[None]], 0)
    planes = shifted(joined[:, :3], "gx", -1)
    longer = jnp.concatenate([joined, planes], 1)
    widened = extended(longer, (("gy", 2),), 3)
    return jnp.pad(widened, ((0, 0), (0, 0), (0, 0), (3, 3)))


def local_forces(widened, displacement, stiffness, damage):
    size_x, size_y, size_z = stiffness.shape
    owned = jnp.zeros((3, size_x, size_y, size_z), jnp.float32)
    reaction = jnp.zeros((3, size_x + 3, size_y + 6, size_z + 6), jnp.float32)
    for index, offset in enumerate(bond_offsets()):
        step_x, step_y, step_z = offset
        window = widened[
            :,
            step_x : step_x + size_x,
            3 + step_y : 3 + step_y + size_y,
            3 + step_z : 3 + step_z + size_z,
        ]
        damage_word = damage[index // 11]
        broken = jnp.bitwise_and(jnp.right_shift(damage_word, index % 11), 1).astype(jnp.float32)
        force = bond_force(displacement, window[:3], stiffness, window[3], broken, offset)
        owned = owned + force
        reaction = reaction - jnp.pad(
            force,
            ((0, 0), (step_x, 3 - step_x), (3 + step_y, 3 - step_y), (3 + step_z, 3 - step_z)),
        )
    return (owned, reaction[..., 3 : 3 + size_z])


def settle_reaction(reaction, size_x, size_y):
    received = shifted(reaction[:, size_x:], "gx", 1)
    middle = reaction[:, :size_x].at[:, :3].add(received)
    upward = shifted(middle[:, :, size_y + 3 :], "gy", 1)
    downward = shifted(middle[:, :, :3], "gy", -1)
    summed = middle[:, :, 3 : 3 + size_y]
    summed = summed.at[:, :, :3].add(upward)
    summed = summed.at[:, :, size_y - 3 :].add(downward)
    return summed


def shards(displacement, velocity, stiffness, damage):
    size_x, size_y, size_z = stiffness.shape
    for iteration in range(STEPS):
        widened = widened_field(displacement, stiffness)
        owned, reaction = local_forces(widened, displacement, stiffness, damage)
        force = owned + settle_reaction(reaction, size_x, size_y)
        velocity = velocity + time_step * force
        displacement = displacement + time_step * velocity
    return (displacement, velocity)


def solution(mesh):
    return jax.shard_map(
        shards,
        mesh=mesh,
        in_specs=(
            P(None, "gx", "gy", None),
            P(None, "gx", "gy", None),
            P("gx", "gy", None),
            P(None, "gx", "gy", None),
        ),
        out_specs=(P(None, "gx", "gy", None), P(None, "gx", "gy", None)),
        check_vma=False,
    )
```

profile of v0, /device:TPU:153, one launch (start us, length us, event | category | flops | bytes accessed | tf_op | source)
XLA Modules:
  0.0 154.5 jit_solution(13486845049916231632)
XLA Ops:
  0.6 0.8 pad_maximum_fusion.9
  1.5 3.9 %collective-permute-start = (f32[4,3,8,128]{3,2,1,0:T(8,128)S(1)}, f32[4,3,8,128]{3,2,1,0:T(8,128)S(1)}, u32[]{:S(2)}, u32[]{:S(2)}) collective-permute-start(f32[4,3,8,128]{3,2,1,0:T(8,128)S(1)} %pad_maximum_fusion.9), channel_id=1, source_target_pairs={{16,0},{32,16},{48,32},{64,48},{80,64},{96,80},{112,96},{128,112},... | collective-permute-start | bytes 147464 | tf_op jit(solution)/shard_map/ppermute | solution.py:18
  5.4 1.2 collective-permute-done
  6.6 3.5 %collective-permute-start.2 = (f32[4,7,3,128]{3,2,1,0:T(4,128)S(1)}, f32[4,7,3,128]{3,2,1,0:T(4,128)S(1)}, u32[]{:S(2)}, u32[]{:S(2)}) collective-permute-start(f32[4,7,3,128]{3,2,1,0:T(4,128)S(1)} %get-tuple-element.454), channel_id=1, source_target_pairs={{1,0},{2,1},{3,2},{4,3},{5,4},{6,5},{7,6},{8,7},{9,8},{10,9},{11,1... | collective-permute-start | bytes 129032 | tf_op jit(solution)/shard_map/ppermute | solution.py:29
  10.1 12.9 %collective-permute-start.1 = (f32[4,7,3,128]{3,2,1,0:T(4,128)S(1)}, f32[4,7,3,128]{3,2,1,0:T(4,128)S(1)}, u32[]{:S(2)}, u32[]{:S(2)}) collective-permute-start(f32[4,7,3,128]{3,2,1,0:T(4,128)S(1)} %get-tuple-element.455), channel_id=1, source_target_pairs={{0,1},{1,2},{2,3},{3,4},{4,5},{5,6},{6,7},{7,8},{8,9},{9,10},{10,1... | collective-permute-start | bytes 129032 | tf_op jit(solution)/shard_map/ppermute | solution.py:28
  23.0 1.2 collective-permute-done.2
  24.3 1.1 collective-permute-done.1
  25.4 0.6 copy-done.54
  26.2 0.8 copy-done.2
  27.4 0.5 copy-done.17
  30.7 0.5 copy-done.6
  35.3 3.2 %pad_subtract_fusion.1 = f32[3,7,14,134]{3,2,1,0:T(8,128)S(1)} fusion(f32[3,4,8,128]{3,2,1,0:T(8,128)S(1)} %get-tuple-element.445, f32[3,4,8,128]{3,2,1,0:T(8,128)S(1)} %get-tuple-element.413, f32[3,4,8,128]{3,2,1,0:T(8,128)S(1)} %get-tuple-element.393, f32[3,4,8,128]{3,2,1,0:T(8,128)S(1)} %get-tuple-element.408, ...), kind=kLoop, calls=%fused_computation.189 | loop fusion | flops 2403156 | bytes 3155856 | tf_op jit(solution)/shard_map/sub | solution.py:87
  38.6 2.5 %collective-permute-start.3 = (f32[3,3,14,128]{3,2,1,0:T(8,128)S(1)}, f32[3,3,14,128]{3,2,1,0:T(8,128)S(1)}, u32[]{:S(2)}, u32[]{:S(2)}) collective-permute-start(f32[3,3,14,128]{3,2,1,0:T(8,128)S(1)} %slice.1852), channel_id=1, source_target_pairs={{0,16},{16,32},{32,48},{48,64},{64,80},{80,96},{96,112},{112,128},... | collective-permute-start | bytes 193544 | tf_op jit(solution)/shard_map/ppermute | solution.py:18
  41.2 5.8 %collective-permute-done.3 = f32[3,3,14,128]{3,2,1,0:T(8,128)S(1)} collective-permute-done((f32[3,3,14,128]{3,2,1,0:T(8,128)S(1)}, f32[3,3,14,128]{3,2,1,0:T(8,128)S(1)}, u32[]{:S(2)}, u32[]{:S(2)}) %collective-permute-start.3) | collective-permute-done | bytes 64544 | tf_op jit(solution)/shard_map/ppermute | solution.py:18
  47.1 16.5 %collective-permute-start.4 = (f32[3,4,3,128]{3,2,1,0:T(4,128)S(1)}, f32[3,4,3,128]{3,2,1,0:T(4,128)S(1)}, u32[]{:S(2)}, u32[]{:S(2)}) collective-permute-start(f32[3,4,3,128]{3,2,1,0:T(4,128)S(1)} %get-tuple-element.459), channel_id=1, source_target_pairs={{0,1},{1,2},{2,3},{3,4},{4,5},{5,6},{6,7},{7,8},{8,9},{9,10},{10,1... | collective-permute-start | bytes 55304 | tf_op jit(solution)/shard_map/ppermute | solution.py:18
  63.6 1.9 %collective-permute-start.5 = (f32[3,4,3,128]{3,2,1,0:T(4,128)S(1)}, f32[3,4,3,128]{3,2,1,0:T(4,128)S(1)}, u32[]{:S(2)}, u32[]{:S(2)}) collective-permute-start(f32[3,4,3,128]{3,2,1,0:T(4,128)S(1)} %get-tuple-element.458), channel_id=1, source_target_pairs={{1,0},{2,1},{3,2},{4,3},{5,4},{6,5},{7,6},{8,7},{9,8},{10,9},{11,1... | collective-permute-start | bytes 55304 | tf_op jit(solution)/shard_map/ppermute | solution.py:18
  65.7 13.8 %collective-permute-done.5 = f32[3,4,3,128]{3,2,1,0:T(4,128)S(1)} collective-permute-done((f32[3,4,3,128]{3,2,1,0:T(4,128)S(1)}, f32[3,4,3,128]{3,2,1,0:T(4,128)S(1)}, u32[]{:S(2)}, u32[]{:S(2)}) %collective-permute-start.5) | collective-permute-done | bytes 18464 | tf_op jit(solution)/shard_map/ppermute | solution.py:18
  80.0 2.3 %collective-permute-start.6 = (f32[4,3,8,128]{3,2,1,0:T(8,128)S(1)}, f32[4,3,8,128]{3,2,1,0:T(8,128)S(1)}, u32[]{:S(2)}, u32[]{:S(2)}) collective-permute-start(f32[4,3,8,128]{3,2,1,0:T(8,128)S(1)} %pad_maximum_fusion.8), channel_id=1, source_target_pairs={{16,0},{32,16},{48,32},{64,48},{80,64},{96,80},{112,96},{128,112},... | collective-permute-start | bytes 147464 | tf_op jit(solution)/shard_map/ppermute | solution.py:18
  82.4 2.5 %collective-permute-done.6 = f32[4,3,8,128]{3,2,1,0:T(8,128)S(1)} collective-permute-done((f32[4,3,8,128]{3,2,1,0:T(8,128)S(1)}, f32[4,3,8,128]{3,2,1,0:T(8,128)S(1)}, u32[]{:S(2)}, u32[]{:S(2)}) %collective-permute-start.6) | collective-permute-done | bytes 49184 | tf_op jit(solution)/shard_map/ppermute | solution.py:18
  84.9 1.9 %collective-permute-start.8 = (f32[4,7,3,128]{3,2,1,0:T(4,128)S(1)}, f32[4,7,3,128]{3,2,1,0:T(4,128)S(1)}, u32[]{:S(2)}, u32[]{:S(2)}) collective-permute-start(f32[4,7,3,128]{3,2,1,0:T(4,128)S(1)} %get-tuple-element.449), channel_id=1, source_target_pairs={{1,0},{2,1},{3,2},{4,3},{5,4},{6,5},{7,6},{8,7},{9,8},{10,9},{11,1... | collective-permute-start | bytes 129032 | tf_op jit(solution)/shard_map/ppermute | solution.py:29
  86.8 14.6 %collective-permute-start.7 = (f32[4,7,3,128]{3,2,1,0:T(4,128)S(1)}, f32[4,7,3,128]{3,2,1,0:T(4,128)S(1)}, u32[]{:S(2)}, u32[]{:S(2)}) collective-permute-start(f32[4,7,3,128]{3,2,1,0:T(4,128)S(1)} %get-tuple-element.450), channel_id=1, source_target_pairs={{0,1},{1,2},{2,3},{3,4},{4,5},{5,6},{6,7},{7,8},{8,9},{9,10},{10,1... | collective-permute-start | bytes 129032 | tf_op jit(solution)/shard_map/ppermute | solution.py:28
  101.5 1.0 collective-permute-done.7
  103.8 0.4 copy-done.53
  104.7 0.6 copy-done.61
  105.5 0.6 copy-done.63
  109.3 3.2 %pad_subtract_fusion = f32[3,7,14,134]{3,2,1,0:T(8,128)S(1)} fusion(f32[3,4,8,128]{3,2,1,0:T(8,128)S(1)} %get-tuple-element.442, f32[3,4,8,128]{3,2,1,0:T(8,128)S(1)} %get-tuple-element.356, f32[3,4,8,128]{3,2,1,0:T(8,128)S(1)} %get-tuple-element.336, f32[3,4,8,128]{3,2,1,0:T(8,128)S(1)} %get-tuple-element.351, f32[3,4,8,128]{3,2,1,0:T(8,128)S(1)} %get-tuple-element.325, ...), kind=kLoop, calls=%fused_computation.188 | loop fusion | flops 2403156 | bytes 3155856 | tf_op jit(solution)/shard_map/sub | solution.py:87
  112.6 1.9 %collective-permute-start.9 = (f32[3,3,14,128]{3,2,1,0:T(8,128)S(1)}, f32[3,3,14,128]{3,2,1,0:T(8,128)S(1)}, u32[]{:S(2)}, u32[]{:S(2)}) collective-permute-start(f32[3,3,14,128]{3,2,1,0:T(8,128)S(1)} %slice.1890), channel_id=1, source_target_pairs={{0,16},{16,32},{32,48},{48,64},{64,80},{80,96},{96,112},{112,128},... | collective-permute-start | bytes 193544 | tf_op jit(solution)/shard_map/ppermute | solution.py:18
  114.6 6.4 %collective-permute-done.9 = f32[3,3,14,128]{3,2,1,0:T(8,128)S(1)} collective-permute-done((f32[3,3,14,128]{3,2,1,0:T(8,128)S(1)}, f32[3,3,14,128]{3,2,1,0:T(8,128)S(1)}, u32[]{:S(2)}, u32[]{:S(2)}) %collective-permute-start.9) | collective-permute-done | bytes 64544 | tf_op jit(solution)/shard_map/ppermute | solution.py:18
  121.1 16.2 %collective-permute-start.10 = (f32[3,4,3,128]{3,2,1,0:T(4,128)S(1)}, f32[3,4,3,128]{3,2,1,0:T(4,128)S(1)}, u32[]{:S(2)}, u32[]{:S(2)}) collective-permute-start(f32[3,4,3,128]{3,2,1,0:T(4,128)S(1)} %get-tuple-element.457), channel_id=1, source_target_pairs={{0,1},{1,2},{2,3},{3,4},{4,5},{5,6},{6,7},{7,8},{8,9},{9,10},{10,1... | collective-permute-start | bytes 55304 | tf_op jit(solution)/shard_map/ppermute | solution.py:18
  137.4 1.9 %collective-permute-start.11 = (f32[3,4,3,128]{3,2,1,0:T(4,128)S(1)}, f32[3,4,3,128]{3,2,1,0:T(4,128)S(1)}, u32[]{:S(2)}, u32[]{:S(2)}) collective-permute-start(f32[3,4,3,128]{3,2,1,0:T(4,128)S(1)} %get-tuple-element.456), channel_id=1, source_target_pairs={{1,0},{2,1},{3,2},{4,3},{5,4},{6,5},{7,6},{8,7},{9,8},{10,9},{11,1... | collective-permute-start | bytes 55304 | tf_op jit(solution)/shard_map/ppermute | solution.py:18
  139.5 13.9 %collective-permute-done.11 = f32[3,4,3,128]{3,2,1,0:T(4,128)S(1)} collective-permute-done((f32[3,4,3,128]{3,2,1,0:T(4,128)S(1)}, f32[3,4,3,128]{3,2,1,0:T(4,128)S(1)}, u32[]{:S(2)}, u32[]{:S(2)}) %collective-permute-start.11) | collective-permute-done | bytes 18464 | tf_op jit(solution)/shard_map/ppermute | solution.py:18
  153.5 1.0 multiply_add_fusion
  (230 shorter events, 13.5 us)
Async XLA Ops:
  0.6 5.9 %copy-start = (f32[3,4,8,128]{3,2,1,0:T(8,128)S(1)}, f32[3,4,8,128]{3,2,1,0:T(8,128)}, u32[]{:S(2)}) copy-start(f32[3,4,8,128]{3,2,1,0:T(8,128)} %param.138) | copy-start | bytes 147460
  0.6 5.9 %copy-start.1 = (f32[4,8,128]{2,1,0:T(8,128)S(1)}, f32[4,8,128]{2,1,0:T(8,128)}, u32[]{:S(2)}) copy-start(f32[4,8,128]{2,1,0:T(8,128)} %param.140) | copy-start | bytes 49156
  1.5 5.1 %collective-permute-start = (f32[4,3,8,128]{3,2,1,0:T(8,128)S(1)}, f32[4,3,8,128]{3,2,1,0:T(8,128)S(1)}, u32[]{:S(2)}, u32[]{:S(2)}) collective-permute-start(f32[4,3,8,128]{3,2,1,0:T(8,128)S(1)} %pad_maximum_fusion.9), channel_id=1, source_target_pairs={{16,0},{32,16},{48,32},{64,48},{80,64},{96,80},{112,96},{128,112},... | collective-permute-start | bytes 147464 | tf_op jit(solution)/shard_map/ppermute | solution.py:18
  6.6 17.6 %collective-permute-start.2 = (f32[4,7,3,128]{3,2,1,0:T(4,128)S(1)}, f32[4,7,3,128]{3,2,1,0:T(4,128)S(1)}, u32[]{:S(2)}, u32[]{:S(2)}) collective-permute-start(f32[4,7,3,128]{3,2,1,0:T(4,128)S(1)} %get-tuple-element.454), channel_id=1, source_target_pairs={{1,0},{2,1},{3,2},{4,3},{5,4},{6,5},{7,6},{8,7},{9,8},{10,9},{11,1... | collective-permute-start | bytes 129032 | tf_op jit(solution)/shard_map/ppermute | solution.py:29
  10.1 15.3 %collective-permute-start.1 = (f32[4,7,3,128]{3,2,1,0:T(4,128)S(1)}, f32[4,7,3,128]{3,2,1,0:T(4,128)S(1)}, u32[]{:S(2)}, u32[]{:S(2)}) collective-permute-start(f32[4,7,3,128]{3,2,1,0:T(4,128)S(1)} %get-tuple-element.455), channel_id=1, source_target_pairs={{0,1},{1,2},{2,3},{3,4},{4,5},{5,6},{6,7},{7,8},{8,9},{9,10},{10,1... | collective-permute-start | bytes 129032 | tf_op jit(solution)/shard_map/ppermute | solution.py:28
  25.3 0.7 copy-start.58
  25.3 0.7 copy-start.60
  26.1 0.9 copy-start.2
  27.3 0.7 copy-start.68
  27.3 0.7 copy-start.70
  28.3 0.7 copy-start.50
  28.3 0.7 copy-start.72
  30.6 0.7 copy-start.51
  31.6 0.7 copy-start.34
  32.3 0.7 copy-start.20
  32.3 0.7 copy-start.21
  32.3 0.7 copy-start.22
  32.3 0.7 copy-start.23
  32.3 0.7 copy-start.27
  32.3 0.7 copy-start.28
  32.3 0.7 copy-start.52
  38.6 8.4 %collective-permute-start.3 = (f32[3,3,14,128]{3,2,1,0:T(8,128)S(1)}, f32[3,3,14,128]{3,2,1,0:T(8,128)S(1)}, u32[]{:S(2)}, u32[]{:S(2)}) collective-permute-start(f32[3,3,14,128]{3,2,1,0:T(8,128)S(1)} %slice.1852), channel_id=1, source_target_pairs={{0,16},{16,32},{32,48},{48,64},{64,80},{80,96},{96,112},{112,128},... | collective-permute-start | bytes 193544 | tf_op jit(solution)/shard_map/ppermute | solution.py:18
  47.1 18.4 %collective-permute-start.4 = (f32[3,4,3,128]{3,2,1,0:T(4,128)S(1)}, f32[3,4,3,128]{3,2,1,0:T(4,128)S(1)}, u32[]{:S(2)}, u32[]{:S(2)}) collective-permute-start(f32[3,4,3,128]{3,2,1,0:T(4,128)S(1)} %get-tuple-element.459), channel_id=1, source_target_pairs={{0,1},{1,2},{2,3},{3,4},{4,5},{5,6},{6,7},{7,8},{8,9},{9,10},{10,1... | collective-permute-start | bytes 55304 | tf_op jit(solution)/shard_map/ppermute | solution.py:18
  63.6 16.0 %collective-permute-start.5 = (f32[3,4,3,128]{3,2,1,0:T(4,128)S(1)}, f32[3,4,3,128]{3,2,1,0:T(4,128)S(1)}, u32[]{:S(2)}, u32[]{:S(2)}) collective-permute-start(f32[3,4,3,128]{3,2,1,0:T(4,128)S(1)} %get-tuple-element.458), channel_id=1, source_target_pairs={{1,0},{2,1},{3,2},{4,3},{5,4},{6,5},{7,6},{8,7},{9,8},{10,9},{11,1... | collective-permute-start | bytes 55304 | tf_op jit(solution)/shard_map/ppermute | solution.py:18
  65.7 14.0 %copy-start.3 = (f32[3,4,8,128]{3,2,1,0:T(8,128)S(1)}, f32[3,4,8,128]{3,2,1,0:T(8,128)}, u32[]{:S(2)}) copy-start(f32[3,4,8,128]{3,2,1,0:T(8,128)} %param.139) | copy-start | bytes 147460
  80.0 4.8 %collective-permute-start.6 = (f32[4,3,8,128]{3,2,1,0:T(8,128)S(1)}, f32[4,3,8,128]{3,2,1,0:T(8,128)S(1)}, u32[]{:S(2)}, u32[]{:S(2)}) collective-permute-start(f32[4,3,8,128]{3,2,1,0:T(8,128)S(1)} %pad_maximum_fusion.8), channel_id=1, source_target_pairs={{16,0},{32,16},{48,32},{64,48},{80,64},{96,80},{112,96},{128,112},... | collective-permute-start | bytes 147464 | tf_op jit(solution)/shard_map/ppermute | solution.py:18
  84.9 16.6 %collective-permute-start.8 = (f32[4,7,3,128]{3,2,1,0:T(4,128)S(1)}, f32[4,7,3,128]{3,2,1,0:T(4,128)S(1)}, u32[]{:S(2)}, u32[]{:S(2)}) collective-permute-start(f32[4,7,3,128]{3,2,1,0:T(4,128)S(1)} %get-tuple-element.449), channel_id=1, source_target_pairs={{1,0},{2,1},{3,2},{4,3},{5,4},{6,5},{7,6},{8,7},{9,8},{10,9},{11,1... | collective-permute-start | bytes 129032 | tf_op jit(solution)/shard_map/ppermute | solution.py:29
  86.8 15.8 %copy-start.73 = (f32[3]{0:T(128)S(1)}, f32[3]{0:T(128)}, u32[]{:S(2)}) copy-start(f32[3]{0:T(128)} %constant.484.clone) | copy-start | bytes 40
  86.8 15.7 %collective-permute-start.7 = (f32[4,7,3,128]{3,2,1,0:T(4,128)S(1)}, f32[4,7,3,128]{3,2,1,0:T(4,128)S(1)}, u32[]{:S(2)}, u32[]{:S(2)}) collective-permute-start(f32[4,7,3,128]{3,2,1,0:T(4,128)S(1)} %get-tuple-element.450), channel_id=1, source_target_pairs={{0,1},{1,2},{2,3},{3,4},{4,5},{5,6},{6,7},{7,8},{8,9},{9,10},{10,1... | collective-permute-start | bytes 129032 | tf_op jit(solution)/shard_map/ppermute | solution.py:28
  112.6 8.4 %collective-permute-start.9 = (f32[3,3,14,128]{3,2,1,0:T(8,128)S(1)}, f32[3,3,14,128]{3,2,1,0:T(8,128)S(1)}, u32[]{:S(2)}, u32[]{:S(2)}) collective-permute-start(f32[3,3,14,128]{3,2,1,0:T(8,128)S(1)} %slice.1890), channel_id=1, source_target_pairs={{0,16},{16,32},{32,48},{48,64},{64,80},{80,96},{96,112},{112,128},... | collective-permute-start | bytes 193544 | tf_op jit(solution)/shard_map/ppermute | solution.py:18
  121.1 18.2 %collective-permute-start.10 = (f32[3,4,3,128]{3,2,1,0:T(4,128)S(1)}, f32[3,4,3,128]{3,2,1,0:T(4,128)S(1)}, u32[]{:S(2)}, u32[]{:S(2)}) collective-permute-start(f32[3,4,3,128]{3,2,1,0:T(4,128)S(1)} %get-tuple-element.457), channel_id=1, source_target_pairs={{0,1},{1,2},{2,3},{3,4},{4,5},{5,6},{6,7},{7,8},{8,9},{9,10},{10,1... | collective-permute-start | bytes 55304 | tf_op jit(solution)/shard_map/ppermute | solution.py:18
  137.4 16.0 %collective-permute-start.11 = (f32[3,4,3,128]{3,2,1,0:T(4,128)S(1)}, f32[3,4,3,128]{3,2,1,0:T(4,128)S(1)}, u32[]{:S(2)}, u32[]{:S(2)}) collective-permute-start(f32[3,4,3,128]{3,2,1,0:T(4,128)S(1)} %get-tuple-element.456), channel_id=1, source_target_pairs={{1,0},{2,1},{3,2},{4,3},{5,4},{6,5},{7,6},{8,7},{9,8},{10,9},{11,1... | collective-permute-start | bytes 55304 | tf_op jit(solution)/shard_map/ppermute | solution.py:18
  (54 other events, 36.0 us)
where the time goes:
time: 155 us; the launch traced here: 154 us
  starting transfers between devices  80.2 us (52%)
  waiting for transfers between devices  46.9 us (30%)
  other arithmetic  17.3 us (11%)
  local copies, waits for them, and re-layouts  8.28 us (5%)
  between operations  1.77 us (1%)
    ppermute x8, starting transfers between devices, shifted(): return lax.ppermute(block, axis, route)  47.2 us
    ppermute x8, waiting for transfers between devices, shifted(): return lax.ppermute(block, axis, route)  43.6 us
    ppermute x2, starting transfers between devices, extended(): before = lax.ppermute(last, axis, up)  27.6 us
    unnamed x148, local copies, waits for them, and re-layouts  7.28 us
    sub x2, other arithmetic, local_forces(): reaction - jnp.pad(force, ((0, 0), (step_x, 3 - step_x), (3 + step_y, 3 -...  6.39 us
    ppermute x2, starting transfers between devices, extended(): after = lax.ppermute(initial, axis, down)  5.39 us
    mul x22, other arithmetic, bond_force(): return factor[None] * separation  3.27 us
  transfers between devices with their start and end apart: 12, of which 9 were waited for; matrix products, arithmetic and copies ran while one was open for 0% of the time, Pallas kernels for 0%

commit v1 on v0

v1 whole, which is shorter than its diff:
```python
import math

import jax
import jax.numpy as jnp
from jax import lax
from jax.experimental import pallas as pl
from jax.experimental.pallas import tpu as pltpu
from jax.sharding import PartitionSpec as P

STEPS = 2

time_step = 0.02
bond_scale = 100.0

PLANES, ROWS = 10, 16
LOW = 3
V, K, D, FIELD_COUNT = 3, 6, 7, 13
ROLLS = (-2, -1, 1, 2)


def bond_offsets():
    table = []
    for step_x in range(0, 4):
        for step_y in range(-3, 4):
            for step_z in range(-3, 4):
                if step_x * step_x + step_y * step_y + step_z * step_z <= 9 and (
                    step_x,
                    step_y,
                    step_z,
                ) > (0, 0, 0):
                    table.append((step_x, step_y, step_z))
    return table


BONDS = list(enumerate(bond_offsets()))

RIGHT_WORDS = [(3, 2, w) for w in range(1, 6)] + [(2, 1, w) for w in range(3, 6)] + [(1, 0, 5)]


def y_slots(upward):
    slots = []
    place = 0

    def put(kind, comp, depth, plane, count):
        nonlocal place
        here = LOW + 7 - depth if upward else LOW + depth
        there = LOW - 1 - depth if upward else LOW + 8 + depth
        slots.append((kind, comp, here, there, plane, count, place))
        place += count

    for kind, comps in (("u", 3), ("s", 1)):
        for comp in range(comps):
            for depth in range(3):
                put(kind, comp, depth, *((1, 8) if depth < 2 else (3, 4)))
    for comp in range(3):
        for depth in range(3):
            put("d", comp, depth, 3, 4)
    words = ((0, 1, 2, 3, 4, 5), (0, 1, 3, 5), (1,)) if upward else ((1, 2, 3, 4), (1, 3))
    for depth, row_words in enumerate(words):
        for word in row_words:
            put("w", word, depth, *((3, 4) if upward and word < 2 else (1, 6)))
    return slots, place


UP_SLOTS, UP_ROWS = y_slots(True)
DOWN_SLOTS, DOWN_ROWS = y_slots(False)
Y_ROWS = -(-max(UP_ROWS, DOWN_ROWS) // 8) * 8

CORNER_ROWS = (1, 2, 11, 12)


def line_of(row):
    return {0: 0, 1: 1, 2: 2, 11: 3, 12: 4, 13: 5, 3: 0, 4: 1, 5: 2, 8: 3, 9: 4, 10: 5}[row]


def spot(ref, plane, row, count=8):
    if ref.shape[-2] == ROWS:
        return (plane, slice(row, row + count))
    return (slice(plane * ROWS + row, plane * ROWS + row + count),)


def rolled(value, distance):
    return pltpu.roll(value, (-distance) % 128, value.ndim - 1)


def lane_mask(distance):
    lane = lax.broadcasted_iota(jnp.int32, (8, 128), 1)
    return lane < 128 - distance if distance > 0 else lane >= -distance


def roll_field(source, target, planes, halves=(0, 8)):
    for c in range(3):
        for plane in planes:
            for half in halves:
                value = source[(c,) + spot(source, plane, half)]
                for i, ez in enumerate(ROLLS):
                    target[(c, i) + spot(target, plane, half)] = rolled(value, ez)


def roll_stiffness(source, target, planes, halves=(0, 8)):
    for plane in planes:
        for half in halves:
            value = source[spot(source, plane, half)]
            for i, ez in enumerate(ROLLS):
                moved = jnp.where(lane_mask(ez), rolled(value, ez), 0.0)
                target[(i,) + spot(target, plane, half)] = moved


def add_bond(total, source, target, length, weight):
    sep = [a - b for a, b in zip(source, target)]
    square = sep[0] * sep[0] + sep[1] * sep[1] + sep[2] * sep[2]
    factor = (1.0 / length - lax.rsqrt(square)) * weight
    return [t + factor * p for t, p in zip(total, sep)]


def intact(q, words, value):
    return jnp.where(jnp.bitwise_and(words, 1 << (q % 11)) == 0, value, 0.0)


def rolled_back(part, ez):
    mask = lane_mask(-ez)
    return [jnp.where(mask, rolled(p, -ez), 0.0) for p in part]


def accumulate(plane, base, owned, reacted, u, ur, s, sr, d):
    here = [u[(c,) + spot(u, plane, base)] for c in range(3)]
    total = [jnp.zeros((8, 128), jnp.float32) for _ in range(3)]

    for ez in range(-3, 4):
        for q, (ex, ey, _) in [b for b in owned if b[1][2] == ez]:
            row, at = base + ey, plane + ex
            length = math.sqrt(ex * ex + ey * ey + ez * ez)
            if ez == 0:
                source = [u[(c,) + spot(u, at, row)] for c in range(3)]
                stiff = s[spot(s, at, row)]
            elif abs(ez) < 3:
                i = ROLLS.index(ez)
                source = [ur[(c, i) + spot(ur, at, row)] for c in range(3)]
                stiff = sr[(i,) + spot(sr, at, row)]
            else:
                source = [rolled(h, ez) for h in here]
                stiff = jnp.where(lane_mask(ez), rolled(s[spot(s, at, row)], ez), 0.0)
            target = [h - float(e) for h, e in zip(here, (ex, ey, ez))]
            words = d[(q // 11,) + spot(d, plane, base)]
            total = add_bond(total, source, target, length, intact(q, words, stiff))
        bonds = [b for b in reacted if b[1][2] == ez]
        if not bonds:
            continue
        moved = here if ez == 0 else [rolled(h, ez) for h in here]
        part = total if ez == 0 else [jnp.zeros((8, 128), jnp.float32) for _ in range(3)]
        for q, (ex, ey, _) in bonds:
            row, at = base - ey, plane - ex
            length = math.sqrt(ex * ex + ey * ey + ez * ez)
            source = [u[(c,) + spot(u, at, row)] for c in range(3)]
            target = [h + float(e) for h, e in zip(moved, (ex, ey, ez))]
            stiff = s[spot(s, at, row)]
            words = d[(q // 11,) + spot(d, at, row)]
            part = add_bond(part, source, target, length, intact(q, words, stiff))
        if ez == 0:
            total = part
        else:
            total = [t + p for t, p in zip(total, rolled_back(part, ez))]
    return total


def accumulate_row(row, sources, u, d, other):
    ou, our, os, osr, od, odr = other

    def line(plain, turned, lead, ez, plane, at):
        ref, lead = (plain, lead) if ez == 0 else (turned, lead + (ROLLS.index(ez),))
        return ref[lead + (line_of(at), slice(plane, plane + 8))]

    here = [u[c, line_of(row), 2:10] for c in range(3)]
    total = [jnp.zeros((8, 128), jnp.float32) for _ in range(3)]
    for q, bond in BONDS:
        length = math.sqrt(sum(e * e for e in bond))
        for sign in (1, -1):
            ex, ey, ez = (sign * e for e in bond)
            if row + ey not in sources:
                continue
            plane, at = 2 + ex, row + ey
            source = [line(ou, our, (c,), ez, plane, at) for c in range(3)]
            stiff = line(os, osr, (), ez, plane, at)
            if sign > 0:
                word = d[q // 11, line_of(row), 2:10]
            else:
                word = line(od, odr, (q // 11,), ez, plane, at)
            target = [h - float(e) for h, e in zip(here, (ex, ey, ez))]
            total = add_bond(total, source, target, length, intact(q, word, stiff))
    return [part[0:4] for part in total]


def put_own(fields, u, s, d):
    for x in range(4):
        if u is not None:
            for c in range(3):
                u[(c,) + spot(u, x + 3, LOW)] = fields[c, x]
        if s is not None:
            s[spot(s, x + 3, LOW)] = jnp.sqrt(fields[K, x])
        for w in range(6):
            d[(w,) + spot(d, x + 3, LOW)] = fields[D + w, x].astype(jnp.int32)


def put_zeros(ref, leads, planes, row, count):
    for lead in leads:
        for plane in planes:
            ref[lead + spot(ref, plane, row, count)] = jnp.zeros((count, 128), ref.dtype)


def put_sides(even, near, far, u, s, d):
    rows = slice(LOW, LOW + 8)

    def left(i):
        return jnp.where(even, far[i], near[i])

    def right(i):
        return jnp.where(even, near[i], far[i])

    for plane in range(3):
        for c in range(3):
            if u is not None:
                u[(c,) + spot(u, plane, LOW)] = left(3 * c + plane)
                u[(c,) + spot(u, 7 + plane, LOW)] = right(3 * c + plane)
        s[spot(s, plane, LOW)] = jnp.sqrt(left(9 + plane))
        s[spot(s, 7 + plane, LOW)] = jnp.sqrt(right(9 + plane))
    for i, (_, plane, word) in enumerate(RIGHT_WORDS):
        d[(word,) + spot(d, plane, LOW)] = left(12 + i).astype(jnp.int32)


def message_lines(even, a, b):
    for slots, above in ((DOWN_SLOTS, True), (UP_SLOTS, False)):
        for slot in slots:
            place, count = slot[6], slot[5]
            one, two = a[place : place + count], b[place : place + count]
            yield slot, jnp.where(even, one, two) if above else jnp.where(even, two, one)


def put_lines(even, a, b, u, s, d, edge):
    for (kind, comp, _, there, plane, count, _), value in message_lines(even, a, b):
        at, planes = line_of(there), slice(plane - 1, plane - 1 + count)
        if kind == "u":
            u[comp, at, planes] = value
        elif kind == "s":
            s[at, planes] = value
        elif kind == "d":
            edge[comp, at, 0:4] = value
        else:
            d[comp, at, planes] = value.astype(jnp.int32)


def put_rows(even, a, b, s, d, wanted):
    for (kind, comp, _, there, plane, count, _), value in message_lines(even, a, b):
        for i in range(count):
            if (plane + i in wanted) and kind == "s":
                s[spot(s, plane + i, there, 1)] = value[i : i + 1]
            elif (plane + i in wanted) and kind == "w":
                d[(comp,) + spot(d, plane + i, there, 1)] = value[i : i + 1].astype(jnp.int32)


def even_place():
    return tuple(lax.axis_index(axis) % 2 == 0 for axis in ("gx", "gy"))


def joined_fields(displacement, velocity, stiffness, damage):
    parts = (displacement, velocity, stiffness[None], damage.astype(jnp.float32))
    total, before = 0.0, 0
    for part in parts:
        count = part.shape[0]
        widths = ((before, FIELD_COUNT - before - count, 0),) + ((0, 0, 0),) * 3
        total = total + lax.pad(part, jnp.float32(0), widths)
        before += count
    return total


def pack_x(fields, far, near):
    even, _ = even_place()
    for i, field in enumerate((0, 1, 2, K)):
        for plane in range(3):
            one, two = fields[field, plane + 1], fields[field, plane]
            near[3 * i + plane] = jnp.where(even, one, two)
            far[3 * i + plane] = jnp.where(even, two, one)
    for i, (plane, _, word) in enumerate(RIGHT_WORDS):
        near[12 + i] = fields[D + word, plane]
        far[12 + i] = fields[D + word, plane]


SIDES = (0, 1, 2, 7, 8, 9)
OUTER = ((0, LOW), (LOW + 8, ROWS - LOW - 8))
EACH = ((0,), (1,), (2,))


def own_part(u, ur, s, sr, d, force):
    roll_field(u, ur, range(3, 7))
    roll_stiffness(s, sr, range(3, 7))
    for i in range(4):
        for plane in (7, 8):
            put_zeros(ur, [(c, i) for c in range(3)], (plane,), 0, ROWS)
            put_zeros(sr, [(i,)], (plane,), 0, ROWS)

    @pl.loop(0, 4)
    def _(x):
        total = accumulate(x + 3, LOW, BONDS, BONDS, u, ur, s, sr, d)
        for c in range(3):
            force[c, x] = total[c]


def side_part(x, u, ur, s, sr, d):
    owned = [b for b in BONDS if x + b[1][0] > 3]
    reacted = [b for b in BONDS if x - b[1][0] < 0]
    return accumulate(x + 3, LOW, owned, reacted, u, ur, s, sr, d)


def first_own(fields, force, u, ur, s, sr, d):
    put_zeros(u, EACH, SIDES, 0, ROWS)
    put_zeros(s, [()], SIDES, 0, ROWS)
    for row, count in OUTER:
        put_zeros(u, EACH, range(3, 7), row, count)
        put_zeros(s, [()], range(3, 7), row, count)
        put_zeros(d, [(w,) for w in range(6)], range(3, 7), row, count)
    put_own(fields, u, s, d)
    own_part(u, ur, s, sr, d, force)


def first_sides(fields, far_x, near_x, force, b, a, v_part, u, ur, s, sr, d, near, up, down):
    even_x, even = even_place()
    for row, count in OUTER:
        put_zeros(u, EACH, SIDES, row, count)
        put_zeros(s, [()], SIDES, row, count)
    put_own(fields, u, s, d)
    put_sides(even_x, near_x, far_x, u, s, d)
    roll_field(u, ur, (7, 8))
    roll_stiffness(s, sr, (7, 8))
    for x in range(4):
        total = side_part(x, u, ur, s, sr, d)
        scale = bond_scale * s[spot(s, x + 3, LOW)]
        for c in range(3):
            velocity = fields[V + c, x] + time_step * (scale * (force[c, x] + total[c]))
            v_part[c, x] = velocity
            near[(c,) + spot(u, x + 3, LOW)] = fields[c, x] + time_step * velocity

    for slots, message in ((UP_SLOTS, up), (DOWN_SLOTS, down)):
        for kind, comp, here, _, plane, count, place in slots:
            lines = pl.ds(plane * ROWS + here, count, stride=ROWS)
            if kind == "u":
                value = u[comp, lines]
            elif kind == "s":
                value = s[lines]
            elif kind == "d":
                value = near[comp, lines]
            else:
                value = d[comp, lines].astype(jnp.float32)
            message[place : place + count] = value
    a[...] = jnp.where(even, up[...], down[...])
    b[...] = jnp.where(even, down[...], up[...])


def roll_lines(u, ur, s, sr, d, dr, words):
    for at in range(6):
        for i, ez in enumerate(ROLLS):
            for w in words[at]:
                dr[w, i, at, 0:8] = rolled(d[w, at, 0:8], ez)
            for c in range(3):
                ur[c, i, at, 0:8] = rolled(u[c, at, 0:8], ez)
            sr[i, at, 0:8] = jnp.where(lane_mask(ez), rolled(s[at, 0:8], ez), 0.0)


def second_own(fields, far_x, near_x, u, ur, s, sr, d, dr, whole_u, whole_s, whole_d):
    even_x, _ = even_place()
    put_own(fields, whole_u, whole_s, whole_d)
    put_sides(even_x, near_x, far_x, whole_u, whole_s, whole_d)
    for row in (3, 4, 5, 8, 9, 10):
        at, lines = line_of(row), pl.ds(ROWS + row, 8, stride=ROWS)
        for c in range(3):
            u[c, at, 0:8] = whole_u[c, lines]
        s[at, 0:8] = whole_s[lines]
        for w in range(6):
            d[w, at, 0:8] = whole_d[w, lines]
    roll_lines(u, ur, s, sr, d, dr, [range(6)] * 6)


def second_rows(fields, b, a, v_part, u, ur, s, sr, d, dr, v_out, near, edge, to_far, to_near, hu, hur, hs, hsr, hd, hdr, sums):
    even_x, even = even_place()
    put_lines(even, a, b, hu, hs, hd, edge)
    sent = UP_SLOTS + DOWN_SLOTS
    words = [[k[1] for k in sent if k[0] == "w" and line_of(k[3]) == at] for at in range(6)]
    roll_lines(hu, hur, hs, hsr, hd, hdr, words)
    beside = (u, ur, s, sr, d, dr)
    beyond = (hu, hur, hs, hsr, hd, hdr)
    for row in (3, 4, 5, 8, 9, 10):
        sources = range(0, LOW) if row < LOW + 4 else range(LOW + 8, LOW + 11)
        force = accumulate_row(row, sources, u, d, beyond)
        for c in range(3):
            sums[c, 8 * (row - LOW) : 8 * (row - LOW) + 4] = force[c]
    for c in range(3):
        for row in (6, 7):
            sums[c, 8 * (row - LOW) : 8 * (row - LOW) + 8] = jnp.zeros((8, 128), jnp.float32)
    for row in (0, 1, 2, 11, 12, 13):
        sources = range(LOW, LOW + 3) if row < LOW + 4 else range(LOW + 5, LOW + 8)
        force = accumulate_row(row, sources, hu, hd, beside)
        at = line_of(row)
        scale = (time_step * time_step * bond_scale) * hs[at, 2:6]
        for c in range(3):
            edge[c, at, 0:4] += scale * force[c]
    for x in range(4):
        scale = (time_step * bond_scale) * jnp.sqrt(fields[K, x])
        for c in range(3):
            velocity = v_part[c, x] + scale * sums[c, pl.ds(x, 8, stride=8)]
            v_out[c, x] = velocity
            near[c, x] = fields[c, x] + time_step * velocity

    place = 0
    for c in range(3):
        for plane in range(3):
            one, two = near[c, plane + 1], near[c, plane]
            to_near[place : place + 8] = jnp.where(even_x, one, two)
            to_far[place : place + 8] = jnp.where(even_x, two, one)
            place += 8
    for c in range(3):
        for row in CORNER_ROWS:
            one, two = edge[c, line_of(row), 2:4], edge[c, line_of(row), 0:2]
            to_near[place : place + 2] = jnp.where(even_x, one, two)
            to_far[place : place + 2] = jnp.where(even_x, two, one)
            place += 2


def last_own(fields, far_x, near_x, b, a, near, edge, force, s, sr, d, u, ur):
    even_x, even = even_place()
    put_zeros(u, EACH, SIDES, 0, ROWS)
    put_zeros(s, [()], SIDES, 0, ROWS)
    put_own(fields, None, s, d)
    put_rows(even, a, b, s, d, range(3, 7))
    for c in range(3):
        u[c, 3:7, LOW : LOW + 8] = near[c]
        for row in (0, 1, 2, 11, 12, 13):
            for x in range(4):
                u[c, x + 3, row : row + 1] = edge[c, line_of(row), x : x + 1]
    own_part(u, ur, s, sr, d, force)
    put_sides(even_x, near_x, far_x, None, s, d)
    put_rows(even, a, b, s, d, SIDES)
    roll_stiffness(s, sr, (7, 8))


def last_sides(near, v_in, force, s, sr, d, far_u, near_u, u_out, v_out, u, ur):
    even_x, _ = even_place()
    for c in range(3):
        u[c, 3:7, LOW : LOW + 8] = near[c]
    put_zeros(u, EACH, SIDES, 0, LOW)
    put_zeros(u, EACH, SIDES, LOW + 8, ROWS - LOW - 8)
    place = 0
    for c in range(3):
        for plane in range(3):
            one, two = near_u[place : place + 8], far_u[place : place + 8]
            u[c, plane, LOW : LOW + 8] = jnp.where(even_x, two, one)
            u[c, 7 + plane, LOW : LOW + 8] = jnp.where(even_x, one, two)
            place += 8
    for c in range(3):
        for row in CORNER_ROWS:
            one, two = near_u[place : place + 2], far_u[place : place + 2]
            before, behind = jnp.where(even_x, two, one), jnp.where(even_x, one, two)
            for plane in range(2):
                u[c, 1 + plane, row : row + 1] = before[plane : plane + 1]
                u[c, 7 + plane, row : row + 1] = behind[plane : plane + 1]
            place += 2
    roll_field(u, ur, (7, 8))
    for x in range(4):
        total = side_part(x, u, ur, s, sr, d)
        scale = bond_scale * s[x + 3, LOW : LOW + 8]
        for c in range(3):
            velocity = v_in[c, x] + time_step * (scale * (force[c, x] + total[c]))
            v_out[c, x] = velocity
            u_out[c, x] = near[c, x] + time_step * velocity


def f32(*shape):
    return jax.ShapeDtypeStruct(shape, jnp.float32)


def arrays(*tail):
    shapes = [f32(3, *tail), f32(3, 4, *tail), f32(*tail), f32(4, *tail)]
    return shapes + [jax.ShapeDtypeStruct((6,) + tail, jnp.int32)]


LAYERS = arrays(PLANES, ROWS, 128)
FLAT = arrays(PLANES * ROWS, 128)
LINES = arrays(6, 16, 128) + [jax.ShapeDtypeStruct((6, 4, 6, 16, 128), jnp.int32)]


def scratch(shapes):
    return [pltpu.VMEM(s.shape, s.dtype) for s in shapes]


def call(kernel, outputs, buffers, *operands, flops=1000):
    return pl.pallas_call(
        kernel,
        out_shape=outputs,
        in_specs=[pl.BlockSpec(memory_space=pltpu.VMEM)] * len(operands),
        out_specs=[pl.BlockSpec(memory_space=pltpu.VMEM)] * len(outputs),
        scratch_shapes=scratch(buffers),
        compiler_params=pltpu.CompilerParams(vmem_limit_bytes=32 * 1024 * 1024),
        cost_estimate=pl.CostEstimate(flops=flops, bytes_accessed=flops, transcendentals=0),
    )(*operands)


def swapped(value, axis, first):
    pairs = [(i, i + 1) for i in range(first, lax.axis_size(axis) - 1, 2)]
    return lax.ppermute(value, axis, pairs + [(j, i) for i, j in pairs])


def shards(displacement, velocity, stiffness, damage):
    point = f32(3, 4, 8, 128)
    edge = f32(3, 6, 8, 128)
    fields = joined_fields(displacement, velocity, stiffness, damage)
    far_x, near_x = call(pack_x, [f32(21, 8, 128)] * 2, [], fields)
    far_x = swapped(far_x, "gx", 1)
    near_x = swapped(near_x, "gx", 0)
    (force,) = call(first_own, [point], LAYERS, fields, flops=4_000_000)
    message = f32(Y_ROWS, 128)
    b, a, v_part = call(
        first_sides, [message, message, point], FLAT + [FLAT[0], message, message], fields, far_x, near_x, force
    )
    b = swapped(b, "gy", 1)
    a = swapped(a, "gy", 0)
    lines = call(second_own, LINES, [FLAT[0], FLAT[2], FLAT[4]], fields, far_x, near_x, flops=2_000_000)
    velocity, near, edge, far_u, near_u = call(
        second_rows,
        [point, point, edge, f32(96, 128), f32(96, 128)],
        LINES + [f32(3, 64, 128)],
        fields,
        b,
        a,
        v_part,
        *lines,
    )
    kept = (fields, far_x, near_x, b, a, near, edge)
    far_u = swapped(far_u.reshape(12, 8, 128), "gx", 1).reshape(96, 128)
    near_u = swapped(near_u.reshape(12, 8, 128), "gx", 0).reshape(96, 128)
    force, *stiff = call(last_own, [point] + LAYERS[2:], LAYERS[:2], *kept, flops=4_000_000)
    return tuple(
        call(last_sides, [point, point], LAYERS[:2], near, velocity, force, *stiff, far_u, near_u)
    )


def solution(mesh):
    return jax.shard_map(
        shards,
        mesh=mesh,
        in_specs=(
            P(None, "gx", "gy", None),
            P(None, "gx", "gy", None),
            P("gx", "gy", None),
            P(None, "gx", "gy", None),
        ),
        out_specs=(P(None, "gx", "gy", None), P(None, "gx", "gy", None)),
        check_vma=False,
    )
```

time: 155 us -> 45.9 us (0.30)
  the two profiles are of different devices: /device:TPU:153 before, /device:TPU:384 now
where the time goes in v1:
time: 45.9 us; the launch traced here: 45.6 us
  starting transfers between devices  19.2 us (42%)
  waiting for transfers between devices  16.6 us (36%)
  Pallas kernels  7.35 us (16%)
  other arithmetic  1.76 us (4%)
  between operations  0.71 us (2%)
    ppermute x6, starting transfers between devices, swapped(): return lax.ppermute(value, axis, pairs + [(j, i) for i, j in pairs])  19.2 us
    ppermute x6, waiting for transfers between devices, swapped(): return lax.ppermute(value, axis, pairs + [(j, i) for i, j in pairs])  16.6 us
    pallas_call x7, Pallas kernels, call(): pl.pallas_call(kernel, out_shape=outputs, in_specs=[pl.BlockSpec(memory_s...  7.35 us
  transfers between devices with their start and end apart: 6, of which 4 were waited for; matrix products, arithmetic and copies ran while one was open for 0% of the time, Pallas kernels for 10%

profile of v1, /device:TPU:384, one launch (start us, length us, event | category | flops | bytes accessed | tf_op | source)
XLA Modules:
  0.0 45.6 jit_solution(18260647981443726283)
XLA Ops:
  0.6 0.9 %convert_element_type.3 = f32[6,4,8,128]{3,2,1,0:T(8,128)S(1)} convert(s32[6,4,8,128]{3,2,1,0:T(8,128)} %param.7) | non-fusion elementwise | flops 24576 | bytes 196608 | tf_op jit(solution)/shard_map/convert_element_type | solution.py:265
  1.5 0.9 %pad_add_fusion.fields = f32[13,4,8,128]{3,2,1,0:T(8,128)S(1)} fusion(f32[6,4,8,128]{3,2,1,0:T(8,128)S(1)} %convert_element_type.3, f32[1,4,8,128]{3,2,1,0:T(8,128)} %bitcast.9, f32[3,4,8,128]{3,2,1,0:T(8,128)} %param.5, f32[3,4,8,128]{3,2,1,0:T(8,128)} %param.4), kind=kLoop, calls=%fused_computation | loop fusion | flops 159744 | bytes 425984 | tf_op jit(solution)/shard_map/add | solution.py:270
  2.4 6.3 %collective-permute-start = (f32[21,8,128]{2,1,0:T(8,128)S(1)}, f32[21,8,128]{2,1,0:T(8,128)S(1)}, u32[]{:S(2)}, u32[]{:S(2)}) collective-permute-start(f32[21,8,128]{2,1,0:T(8,128)S(1)} %get-tuple-element.22), channel_id=1, source_target_pairs={{16,32},{48,64},{80,96},{112,128},{144,160},{176,192},{208,224},{2... | collective-permute-start | bytes 258056 | tf_op jit(solution)/shard_map/ppermute | solution.py:506
  8.8 1.9 %collective-permute-start.1 = (f32[21,8,128]{2,1,0:T(8,128)S(1)}, f32[21,8,128]{2,1,0:T(8,128)S(1)}, u32[]{:S(2)}, u32[]{:S(2)}) collective-permute-start(f32[21,8,128]{2,1,0:T(8,128)S(1)} %get-tuple-element.23), channel_id=1, source_target_pairs={{0,16},{32,48},{64,80},{96,112},{128,144},{160,176},{192,208},{224... | collective-permute-start | bytes 258056 | tf_op jit(solution)/shard_map/ppermute | solution.py:506
  10.7 2.1 %shard_map.60.force = f32[3,4,8,128]{3,2,1,0:T(8,128)S(1)} custom-call(f32[13,4,8,128]{3,2,1,0:T(8,128)S(1)} %pad_add_fusion.fields), custom_call_target="tpu_custom_call" | custom-call | flops 4000000 | bytes 4000000 | tf_op jit(solution)/shard_map/pallas_call | solution.py:493
  12.7 0.0 collective-permute-done.far_x
  12.7 2.4 %collective-permute-done.1.near_x = f32[21,8,128]{2,1,0:T(8,128)S(1)} collective-permute-done((f32[21,8,128]{2,1,0:T(8,128)S(1)}, f32[21,8,128]{2,1,0:T(8,128)S(1)}, u32[]{:S(2)}, u32[]{:S(2)}) %collective-permute-start.1) | collective-permute-done | bytes 86048 | tf_op jit(solution)/shard_map/ppermute | solution.py:506
  15.1 0.6 %shard_map.61 = (f32[176,128]{1,0:T(8,128)S(1)}, f32[176,128]{1,0:T(8,128)S(1)}, f32[3,4,8,128]{3,2,1,0:T(8,128)S(1)}) custom-call(f32[13,4,8,128]{3,2,1,0:T(8,128)S(1)} %pad_add_fusion.fields, f32[21,8,128]{2,1,0:T(8,128)S(1)} %collective-permute-done.far_x, f32[21,8,128]{2,1,0:T(8,128)S(1)} %collective-permute-done.1.near_x, ...), custom_call_target="tpu_custom_call" | custom-call | flops 1000 | bytes 1000 | tf_op jit(solution)/shard_map/pallas_call | solution.py:493
  15.7 2.3 %collective-permute-start.2 = (f32[176,128]{1,0:T(8,128)S(1)}, f32[176,128]{1,0:T(8,128)S(1)}, u32[]{:S(2)}, u32[]{:S(2)}) collective-permute-start(f32[176,128]{1,0:T(8,128)S(1)} %get-tuple-element.24), channel_id=1, source_target_pairs={{1,2},{3,4},{5,6},{7,8},{9,10},{11,12},{13,14},{2,1},{4,3},{6,5},{... | collective-permute-start | bytes 270344 | tf_op jit(solution)/shard_map/ppermute | solution.py:506
  18.0 3.2 %collective-permute-start.3 = (f32[176,128]{1,0:T(8,128)S(1)}, f32[176,128]{1,0:T(8,128)S(1)}, u32[]{:S(2)}, u32[]{:S(2)}) collective-permute-start(f32[176,128]{1,0:T(8,128)S(1)} %get-tuple-element.25), channel_id=1, source_target_pairs={{0,1},{2,3},{4,5},{6,7},{8,9},{10,11},{12,13},{14,15},{1,0},{3,2},... | collective-permute-start | bytes 270344 | tf_op jit(solution)/shard_map/ppermute | solution.py:506
  21.2 0.4 shard_map.62
  21.6 12.3 %collective-permute-done.2.b = f32[176,128]{1,0:T(8,128)S(1)} collective-permute-done((f32[176,128]{1,0:T(8,128)S(1)}, f32[176,128]{1,0:T(8,128)S(1)}, u32[]{:S(2)}, u32[]{:S(2)}) %collective-permute-start.2) | collective-permute-done | bytes 90144 | tf_op jit(solution)/shard_map/ppermute | solution.py:506
  33.9 0.0 collective-permute-done.3.a
  33.9 1.0 %shard_map.63 = (f32[3,4,8,128]{3,2,1,0:T(8,128)S(1)}, f32[3,4,8,128]{3,2,1,0:T(8,128)S(1)}, f32[3,6,8,128]{3,2,1,0:T(8,128)S(1)}, f32[96,128]{1,0:T(8,128)S(1)}, f32[96,128]{1,0:T(8,128)S(1)}) custom-call(f32[13,4,8,128]{3,2,1,0:T(8,128)S(1)} %pad_add_fusion.fields, f32[176,128]{1,0:T(8,128)S(1)} %collective-permute-done.2.b, ...), custom_call_target="tpu_custom_call" | custom-call | flops 1000 | bytes 1000 | tf_op jit(solution)/shard_map/pallas_call | solution.py:493
  34.9 3.5 %collective-permute-start.4 = (f32[12,8,128]{2,1,0:T(8,128)S(1)}, f32[12,8,128]{2,1,0:T(8,128)S(1)}, u32[]{:S(2)}, u32[]{:S(2)}) collective-permute-start(f32[12,8,128]{2,1,0:T(8,128)S(1)} %bitcast.8), channel_id=1, source_target_pairs={{16,32},{48,64},{80,96},{112,128},{144,160},{176,192},{208,224},{2... | collective-permute-start | bytes 147464 | tf_op jit(solution)/shard_map/ppermute | solution.py:506
  38.4 1.9 %collective-permute-start.5 = (f32[12,8,128]{2,1,0:T(8,128)S(1)}, f32[12,8,128]{2,1,0:T(8,128)S(1)}, u32[]{:S(2)}, u32[]{:S(2)}) collective-permute-start(f32[12,8,128]{2,1,0:T(8,128)S(1)} %bitcast.7), channel_id=1, source_target_pairs={{0,16},{32,48},{64,80},{96,112},{128,144},{160,176},{192,208},{224... | collective-permute-start | bytes 147464 | tf_op jit(solution)/shard_map/ppermute | solution.py:506
  40.4 2.2 %shard_map.64 = (f32[3,4,8,128]{3,2,1,0:T(8,128)S(1)}, f32[10,16,128]{2,1,0:T(8,128)S(1)}, f32[4,10,16,128]{3,2,1,0:T(8,128)S(1)}, s32[6,10,16,128]{3,2,1,0:T(8,128)S(1)}) custom-call(f32[13,4,8,128]{3,2,1,0:T(8,128)S(1)} %pad_add_fusion.fields, f32[21,8,128]{2,1,0:T(8,128)S(1)} %collective-permute-done.far_x, ...), custom_call_target="tpu_custom_call" | custom-call | flops 4000000 | bytes 4000000 | tf_op jit(solution)/shard_map/pallas_call | solution.py:493
  42.5 1.7 %collective-permute-done.4 = f32[12,8,128]{2,1,0:T(8,128)S(1)} collective-permute-done((f32[12,8,128]{2,1,0:T(8,128)S(1)}, f32[12,8,128]{2,1,0:T(8,128)S(1)}, u32[]{:S(2)}, u32[]{:S(2)}) %collective-permute-start.4) | collective-permute-done | bytes 49184 | tf_op jit(solution)/shard_map/ppermute | solution.py:506
  44.2 0.2 collective-permute-done.5
  44.4 1.2 %shard_map.65 = (f32[3,4,8,128]{3,2,1,0:T(8,128)}, f32[3,4,8,128]{3,2,1,0:T(8,128)}) custom-call(f32[3,4,8,128]{3,2,1,0:T(8,128)S(1)} %get-tuple-element.33.near, f32[3,4,8,128]{3,2,1,0:T(8,128)S(1)} %get-tuple-element.34.v_in, f32[3,4,8,128]{3,2,1,0:T(8,128)S(1)} %get-tuple-element.36.force, f32[10,16,128]{2,1,0:T(8,128)S(1)} %get-tuple-element.37.s, ...), custom_call_target="tpu_custom_call" | custom-call | flops 1000 | bytes 1000 | tf_op jit(solution)/shard_map/pallas_call | solution.py:493
  (1 shorter events, 0.0 us)
Async XLA Ops:
  2.4 10.3 %collective-permute-start = (f32[21,8,128]{2,1,0:T(8,128)S(1)}, f32[21,8,128]{2,1,0:T(8,128)S(1)}, u32[]{:S(2)}, u32[]{:S(2)}) collective-permute-start(f32[21,8,128]{2,1,0:T(8,128)S(1)} %get-tuple-element.22), channel_id=1, source_target_pairs={{16,32},{48,64},{80,96},{112,128},{144,160},{176,192},{208,224},{2... | collective-permute-start | bytes 258056 | tf_op jit(solution)/shard_map/ppermute | solution.py:506
  8.8 6.4 %collective-permute-start.1 = (f32[21,8,128]{2,1,0:T(8,128)S(1)}, f32[21,8,128]{2,1,0:T(8,128)S(1)}, u32[]{:S(2)}, u32[]{:S(2)}) collective-permute-start(f32[21,8,128]{2,1,0:T(8,128)S(1)} %get-tuple-element.23), channel_id=1, source_target_pairs={{0,16},{32,48},{64,80},{96,112},{128,144},{160,176},{192,208},{224... | collective-permute-start | bytes 258056 | tf_op jit(solution)/shard_map/ppermute | solution.py:506
  15.7 18.1 %collective-permute-start.2 = (f32[176,128]{1,0:T(8,128)S(1)}, f32[176,128]{1,0:T(8,128)S(1)}, u32[]{:S(2)}, u32[]{:S(2)}) collective-permute-start(f32[176,128]{1,0:T(8,128)S(1)} %get-tuple-element.24), channel_id=1, source_target_pairs={{1,2},{3,4},{5,6},{7,8},{9,10},{11,12},{13,14},{2,1},{4,3},{6,5},{... | collective-permute-start | bytes 270344 | tf_op jit(solution)/shard_map/ppermute | solution.py:506
  18.0 15.9 %collective-permute-start.3 = (f32[176,128]{1,0:T(8,128)S(1)}, f32[176,128]{1,0:T(8,128)S(1)}, u32[]{:S(2)}, u32[]{:S(2)}) collective-permute-start(f32[176,128]{1,0:T(8,128)S(1)} %get-tuple-element.25), channel_id=1, source_target_pairs={{0,1},{2,3},{4,5},{6,7},{8,9},{10,11},{12,13},{14,15},{1,0},{3,2},... | collective-permute-start | bytes 270344 | tf_op jit(solution)/shard_map/ppermute | solution.py:506
  34.9 9.3 %collective-permute-start.4 = (f32[12,8,128]{2,1,0:T(8,128)S(1)}, f32[12,8,128]{2,1,0:T(8,128)S(1)}, u32[]{:S(2)}, u32[]{:S(2)}) collective-permute-start(f32[12,8,128]{2,1,0:T(8,128)S(1)} %bitcast.8), channel_id=1, source_target_pairs={{16,32},{48,64},{80,96},{112,128},{144,160},{176,192},{208,224},{2... | collective-permute-start | bytes 147464 | tf_op jit(solution)/shard_map/ppermute | solution.py:506
  38.4 6.0 %collective-permute-start.5 = (f32[12,8,128]{2,1,0:T(8,128)S(1)}, f32[12,8,128]{2,1,0:T(8,128)S(1)}, u32[]{:S(2)}, u32[]{:S(2)}) collective-permute-start(f32[12,8,128]{2,1,0:T(8,128)S(1)} %bitcast.7), channel_id=1, source_target_pairs={{0,16},{32,48},{64,80},{96,112},{128,144},{160,176},{192,208},{224... | collective-permute-start | bytes 147464 | tf_op jit(solution)/shard_map/ppermute | solution.py:506

commit v2 on v1

--- a/solution.py
+++ b/solution.py
@@ -262,12 +262,12 @@
 
 
 def joined_fields(displacement, velocity, stiffness, damage):
-    parts = (displacement, velocity, stiffness[None], damage.astype(jnp.float32))
+    parts = (displacement, velocity, stiffness[None], damage)
     total, before = 0.0, 0
     for part in parts:
         count = part.shape[0]
         widths = ((before, FIELD_COUNT - before - count, 0),) + ((0, 0, 0),) * 3
-        total = total + lax.pad(part, jnp.float32(0), widths)
+        total = total + lax.pad(part, part.dtype.type(0), widths).astype(jnp.float32)
         before += count
     return total
 
@@ -440,7 +440,7 @@
     roll_stiffness(s, sr, (7, 8))
 
 
-def last_sides(near, v_in, force, s, sr, d, far_u, near_u, u_out, v_out, u, ur):
+def last_sides(near, v_in, force, s, sr, d, far_u, near_u, u_out, v_out, u, ur, ready, sems):
     even_x, _ = even_place()
     for c in range(3):
         u[c, 3:7, LOW : LOW + 8] = near[c]
@@ -462,13 +462,20 @@
                 u[c, 7 + plane, row : row + 1] = behind[plane : plane + 1]
             place += 2
     roll_field(u, ur, (7, 8))
+    copies = []
     for x in range(4):
         total = side_part(x, u, ur, s, sr, d)
         scale = bond_scale * s[x + 3, LOW : LOW + 8]
         for c in range(3):
             velocity = v_in[c, x] + time_step * (scale * (force[c, x] + total[c]))
-            v_out[c, x] = velocity
-            u_out[c, x] = near[c, x] + time_step * velocity
+            ready[1, c, x] = velocity
+            ready[0, c, x] = near[c, x] + time_step * velocity
+        for i, out in enumerate((u_out, v_out)):
+            copy = pltpu.make_async_copy(ready.at[i, :, x], out.at[:, x], sems.at[i, x])
+            copy.start()
+            copies.append(copy)
+    for copy in copies:
+        copy.wait()
 
 
 def f32(*shape):
@@ -489,13 +496,13 @@
     return [pltpu.VMEM(s.shape, s.dtype) for s in shapes]
 
 
-def call(kernel, outputs, buffers, *operands, flops=1000):
+def call(kernel, outputs, buffers, *operands, flops=1000, space=pltpu.VMEM, extra=()):
     return pl.pallas_call(
         kernel,
         out_shape=outputs,
         in_specs=[pl.BlockSpec(memory_space=pltpu.VMEM)] * len(operands),
-        out_specs=[pl.BlockSpec(memory_space=pltpu.VMEM)] * len(outputs),
-        scratch_shapes=scratch(buffers),
+        out_specs=[pl.BlockSpec(memory_space=space)] * len(outputs),
+        scratch_shapes=scratch(buffers) + list(extra),
         compiler_params=pltpu.CompilerParams(vmem_limit_bytes=32 * 1024 * 1024),
         cost_estimate=pl.CostEstimate(flops=flops, bytes_accessed=flops, transcendentals=0),
     )(*operands)
@@ -536,7 +543,19 @@
     near_u = swapped(near_u.reshape(12, 8, 128), "gx", 0).reshape(96, 128)
     force, *stiff = call(last_own, [point] + LAYERS[2:], LAYERS[:2], *kept, flops=4_000_000)
     return tuple(
-        call(last_sides, [point, point], LAYERS[:2], near, velocity, force, *stiff, far_u, near_u)
+        call(
+            last_sides,
+            [point, point],
+            LAYERS[:2] + [f32(2, 3, 4, 8, 128)],
+            near,
+            velocity,
+            force,
+            *stiff,
+            far_u,
+            near_u,
+            space=pl.ANY,
+            extra=[pltpu.SemaphoreType.DMA((2, 4))],
+        )
     )
 
 

time: 45.9 us -> 45.1 us (0.983)
  other arithmetic: 1.76 us -> 0.91 us
    convert_element_type x1 -> x0, other arithmetic: 0.9 us -> none  [joined_fields(): damage.astype(jnp.float32)]
where the time goes in v2:
time: 45.1 us; the launch traced here: 44.8 us
  starting transfers between devices  19.2 us (43%)
  waiting for transfers between devices  16.6 us (37%)
  Pallas kernels  7.39 us (16%)
  other arithmetic  0.91 us (2%)
  between operations  0.72 us (2%)
    ppermute x6, starting transfers between devices, swapped(): return lax.ppermute(value, axis, pairs + [(j, i) for i, j in pairs])  19.2 us
    ppermute x6, waiting for transfers between devices, swapped(): return lax.ppermute(value, axis, pairs + [(j, i) for i, j in pairs])  16.6 us
    pallas_call x7, Pallas kernels, call(): pl.pallas_call(kernel, out_shape=outputs, in_specs=[pl.BlockSpec(memory_s...  7.39 us
    add x1, other arithmetic, joined_fields(): total + lax.pad(part, part.dtype.type(0), widths).astype(jnp.float32)  0.91 us
  transfers between devices with their start and end apart: 6, of which 4 were waited for; matrix products, arithmetic and copies ran while one was open for 0% of the time, Pallas kernels for 10%

profile of v2, /device:TPU:384, one launch (start us, length us, event | category | flops | bytes accessed | tf_op | source)
XLA Modules:
  0.0 44.8 jit_solution(894399158657507720)
XLA Ops:
  0.6 0.9 %convert_add_fusion.fields = f32[13,4,8,128]{3,2,1,0:T(8,128)S(1)} fusion(s32[6,4,8,128]{3,2,1,0:T(8,128)} %param.7, f32[1,4,8,128]{3,2,1,0:T(8,128)} %bitcast.9, f32[3,4,8,128]{3,2,1,0:T(8,128)} %param.5, f32[3,4,8,128]{3,2,1,0:T(8,128)} %param.4), kind=kLoop, calls=%fused_computation | loop fusion | flops 212992 | bytes 425984 | tf_op jit(solution)/shard_map/add | solution.py:270
  1.6 6.3 %collective-permute-start = (f32[21,8,128]{2,1,0:T(8,128)S(1)}, f32[21,8,128]{2,1,0:T(8,128)S(1)}, u32[]{:S(2)}, u32[]{:S(2)}) collective-permute-start(f32[21,8,128]{2,1,0:T(8,128)S(1)} %get-tuple-element.22), channel_id=1, source_target_pairs={{16,32},{48,64},{80,96},{112,128},{144,160},{176,192},{208,224},{2... | collective-permute-start | bytes 258056 | tf_op jit(solution)/shard_map/ppermute | solution.py:513
  7.9 1.9 %collective-permute-start.1 = (f32[21,8,128]{2,1,0:T(8,128)S(1)}, f32[21,8,128]{2,1,0:T(8,128)S(1)}, u32[]{:S(2)}, u32[]{:S(2)}) collective-permute-start(f32[21,8,128]{2,1,0:T(8,128)S(1)} %get-tuple-element.23), channel_id=1, source_target_pairs={{0,16},{32,48},{64,80},{96,112},{128,144},{160,176},{192,208},{224... | collective-permute-start | bytes 258056 | tf_op jit(solution)/shard_map/ppermute | solution.py:513
  9.8 2.1 %shard_map.60.force = f32[3,4,8,128]{3,2,1,0:T(8,128)S(1)} custom-call(f32[13,4,8,128]{3,2,1,0:T(8,128)S(1)} %convert_add_fusion.fields), custom_call_target="tpu_custom_call" | custom-call | flops 4000000 | bytes 4000000 | tf_op jit(solution)/shard_map/pallas_call | solution.py:500
  11.9 0.0 collective-permute-done.far_x
  11.9 2.4 %collective-permute-done.1.near_x = f32[21,8,128]{2,1,0:T(8,128)S(1)} collective-permute-done((f32[21,8,128]{2,1,0:T(8,128)S(1)}, f32[21,8,128]{2,1,0:T(8,128)S(1)}, u32[]{:S(2)}, u32[]{:S(2)}) %collective-permute-start.1) | collective-permute-done | bytes 86048 | tf_op jit(solution)/shard_map/ppermute | solution.py:513
  14.3 0.6 %shard_map.61 = (f32[176,128]{1,0:T(8,128)S(1)}, f32[176,128]{1,0:T(8,128)S(1)}, f32[3,4,8,128]{3,2,1,0:T(8,128)S(1)}) custom-call(f32[13,4,8,128]{3,2,1,0:T(8,128)S(1)} %convert_add_fusion.fields, f32[21,8,128]{2,1,0:T(8,128)S(1)} %collective-permute-done.far_x, f32[21,8,128]{2,1,0:T(8,128)S(1)} %collective-permute-done.1.near_x, ...), custom_call_target="tpu_custom_call" | custom-call | flops 1000 | bytes 1000 | tf_op jit(solution)/shard_map/pallas_call | solution.py:500
  14.9 2.3 %collective-permute-start.2 = (f32[176,128]{1,0:T(8,128)S(1)}, f32[176,128]{1,0:T(8,128)S(1)}, u32[]{:S(2)}, u32[]{:S(2)}) collective-permute-start(f32[176,128]{1,0:T(8,128)S(1)} %get-tuple-element.24), channel_id=1, source_target_pairs={{1,2},{3,4},{5,6},{7,8},{9,10},{11,12},{13,14},{2,1},{4,3},{6,5},{... | collective-permute-start | bytes 270344 | tf_op jit(solution)/shard_map/ppermute | solution.py:513
  17.2 3.2 %collective-permute-start.3 = (f32[176,128]{1,0:T(8,128)S(1)}, f32[176,128]{1,0:T(8,128)S(1)}, u32[]{:S(2)}, u32[]{:S(2)}) collective-permute-start(f32[176,128]{1,0:T(8,128)S(1)} %get-tuple-element.25), channel_id=1, source_target_pairs={{0,1},{2,3},{4,5},{6,7},{8,9},{10,11},{12,13},{14,15},{1,0},{3,2},... | collective-permute-start | bytes 270344 | tf_op jit(solution)/shard_map/ppermute | solution.py:513
  20.4 0.4 shard_map.62
  20.8 12.3 %collective-permute-done.2.b = f32[176,128]{1,0:T(8,128)S(1)} collective-permute-done((f32[176,128]{1,0:T(8,128)S(1)}, f32[176,128]{1,0:T(8,128)S(1)}, u32[]{:S(2)}, u32[]{:S(2)}) %collective-permute-start.2) | collective-permute-done | bytes 90144 | tf_op jit(solution)/shard_map/ppermute | solution.py:513
  33.0 0.0 collective-permute-done.3.a
  33.0 1.0 %shard_map.63 = (f32[3,4,8,128]{3,2,1,0:T(8,128)S(1)}, f32[3,4,8,128]{3,2,1,0:T(8,128)S(1)}, f32[3,6,8,128]{3,2,1,0:T(8,128)S(1)}, f32[96,128]{1,0:T(8,128)S(1)}, f32[96,128]{1,0:T(8,128)S(1)}) custom-call(f32[13,4,8,128]{3,2,1,0:T(8,128)S(1)} %convert_add_fusion.fields, f32[176,128]{1,0:T(8,128)S(1)} %collective-permute-done.2.b, ...), custom_call_target="tpu_custom_call" | custom-call | flops 1000 | bytes 1000 | tf_op jit(solution)/shard_map/pallas_call | solution.py:500
  34.1 3.5 %collective-permute-start.4 = (f32[12,8,128]{2,1,0:T(8,128)S(1)}, f32[12,8,128]{2,1,0:T(8,128)S(1)}, u32[]{:S(2)}, u32[]{:S(2)}) collective-permute-start(f32[12,8,128]{2,1,0:T(8,128)S(1)} %bitcast.8), channel_id=1, source_target_pairs={{16,32},{48,64},{80,96},{112,128},{144,160},{176,192},{208,224},{2... | collective-permute-start | bytes 147464 | tf_op jit(solution)/shard_map/ppermute | solution.py:513
  37.6 1.9 %collective-permute-start.5 = (f32[12,8,128]{2,1,0:T(8,128)S(1)}, f32[12,8,128]{2,1,0:T(8,128)S(1)}, u32[]{:S(2)}, u32[]{:S(2)}) collective-permute-start(f32[12,8,128]{2,1,0:T(8,128)S(1)} %bitcast.7), channel_id=1, source_target_pairs={{0,16},{32,48},{64,80},{96,112},{128,144},{160,176},{192,208},{224... | collective-permute-start | bytes 147464 | tf_op jit(solution)/shard_map/ppermute | solution.py:513
  39.5 2.2 %shard_map.64 = (f32[3,4,8,128]{3,2,1,0:T(8,128)S(1)}, f32[10,16,128]{2,1,0:T(8,128)S(1)}, f32[4,10,16,128]{3,2,1,0:T(8,128)S(1)}, s32[6,10,16,128]{3,2,1,0:T(8,128)S(1)}) custom-call(f32[13,4,8,128]{3,2,1,0:T(8,128)S(1)} %convert_add_fusion.fields, f32[21,8,128]{2,1,0:T(8,128)S(1)} %collective-permute-done.far_x, ...), custom_call_target="tpu_custom_call" | custom-call | flops 4000000 | bytes 4000000 | tf_op jit(solution)/shard_map/pallas_call | solution.py:500
  41.7 1.7 %collective-permute-done.4 = f32[12,8,128]{2,1,0:T(8,128)S(1)} collective-permute-done((f32[12,8,128]{2,1,0:T(8,128)S(1)}, f32[12,8,128]{2,1,0:T(8,128)S(1)}, u32[]{:S(2)}, u32[]{:S(2)}) %collective-permute-start.4) | collective-permute-done | bytes 49184 | tf_op jit(solution)/shard_map/ppermute | solution.py:513
  43.4 0.2 collective-permute-done.5
  43.6 1.2 %shard_map.65 = (f32[3,4,8,128]{3,2,1,0:T(8,128)}, f32[3,4,8,128]{3,2,1,0:T(8,128)}) custom-call(f32[3,4,8,128]{3,2,1,0:T(8,128)S(1)} %get-tuple-element.33.near, f32[3,4,8,128]{3,2,1,0:T(8,128)S(1)} %get-tuple-element.34.v_in, f32[3,4,8,128]{3,2,1,0:T(8,128)S(1)} %get-tuple-element.36.force, f32[10,16,128]{2,1,0:T(8,128)S(1)} %get-tuple-element.37.s, ...), custom_call_target="tpu_custom_call" | custom-call | flops 1000 | bytes 1000 | tf_op jit(solution)/shard_map/pallas_call | solution.py:500
  (1 shorter events, 0.0 us)
Async XLA Ops:
  1.6 10.3 %collective-permute-start = (f32[21,8,128]{2,1,0:T(8,128)S(1)}, f32[21,8,128]{2,1,0:T(8,128)S(1)}, u32[]{:S(2)}, u32[]{:S(2)}) collective-permute-start(f32[21,8,128]{2,1,0:T(8,128)S(1)} %get-tuple-element.22), channel_id=1, source_target_pairs={{16,32},{48,64},{80,96},{112,128},{144,160},{176,192},{208,224},{2... | collective-permute-start | bytes 258056 | tf_op jit(solution)/shard_map/ppermute | solution.py:513
  7.9 6.4 %collective-permute-start.1 = (f32[21,8,128]{2,1,0:T(8,128)S(1)}, f32[21,8,128]{2,1,0:T(8,128)S(1)}, u32[]{:S(2)}, u32[]{:S(2)}) collective-permute-start(f32[21,8,128]{2,1,0:T(8,128)S(1)} %get-tuple-element.23), channel_id=1, source_target_pairs={{0,16},{32,48},{64,80},{96,112},{128,144},{160,176},{192,208},{224... | collective-permute-start | bytes 258056 | tf_op jit(solution)/shard_map/ppermute | solution.py:513
  14.9 18.1 %collective-permute-start.2 = (f32[176,128]{1,0:T(8,128)S(1)}, f32[176,128]{1,0:T(8,128)S(1)}, u32[]{:S(2)}, u32[]{:S(2)}) collective-permute-start(f32[176,128]{1,0:T(8,128)S(1)} %get-tuple-element.24), channel_id=1, source_target_pairs={{1,2},{3,4},{5,6},{7,8},{9,10},{11,12},{13,14},{2,1},{4,3},{6,5},{... | collective-permute-start | bytes 270344 | tf_op jit(solution)/shard_map/ppermute | solution.py:513
  17.2 15.9 %collective-permute-start.3 = (f32[176,128]{1,0:T(8,128)S(1)}, f32[176,128]{1,0:T(8,128)S(1)}, u32[]{:S(2)}, u32[]{:S(2)}) collective-permute-start(f32[176,128]{1,0:T(8,128)S(1)} %get-tuple-element.25), channel_id=1, source_target_pairs={{0,1},{2,3},{4,5},{6,7},{8,9},{10,11},{12,13},{14,15},{1,0},{3,2},... | collective-permute-start | bytes 270344 | tf_op jit(solution)/shard_map/ppermute | solution.py:513
  34.1 9.3 %collective-permute-start.4 = (f32[12,8,128]{2,1,0:T(8,128)S(1)}, f32[12,8,128]{2,1,0:T(8,128)S(1)}, u32[]{:S(2)}, u32[]{:S(2)}) collective-permute-start(f32[12,8,128]{2,1,0:T(8,128)S(1)} %bitcast.8), channel_id=1, source_target_pairs={{16,32},{48,64},{80,96},{112,128},{144,160},{176,192},{208,224},{2... | collective-permute-start | bytes 147464 | tf_op jit(solution)/shard_map/ppermute | solution.py:513
  37.6 6.0 %collective-permute-start.5 = (f32[12,8,128]{2,1,0:T(8,128)S(1)}, f32[12,8,128]{2,1,0:T(8,128)S(1)}, u32[]{:S(2)}, u32[]{:S(2)}) collective-permute-start(f32[12,8,128]{2,1,0:T(8,128)S(1)} %bitcast.7), channel_id=1, source_target_pairs={{0,16},{32,48},{64,80},{96,112},{128,144},{160,176},{192,208},{224... | collective-permute-start | bytes 147464 | tf_op jit(solution)/shard_map/ppermute | solution.py:513

commit v3 on v1

--- a/solution.py
+++ b/solution.py
@@ -34,7 +34,8 @@
 
 BONDS = list(enumerate(bond_offsets()))
 
-RIGHT_WORDS = [(3, 2, w) for w in range(1, 6)] + [(2, 1, w) for w in range(3, 6)] + [(1, 0, 5)]
+RIGHT_WORDS = [(3, 2, w) for w in range(1, 6)] + [(2, 1, w) for w in range(3, 6)]
+X_TILES = 12 + len(RIGHT_WORDS)
 
 
 def y_slots(upward):
@@ -225,6 +226,7 @@
         s[spot(s, 7 + plane, LOW)] = jnp.sqrt(right(9 + plane))
     for i, (_, plane, word) in enumerate(RIGHT_WORDS):
         d[(word,) + spot(d, plane, LOW)] = left(12 + i).astype(jnp.int32)
+    d[(5,) + spot(d, 0, LOW)] = jnp.zeros((8, 128), jnp.int32)
 
 
 def message_lines(even, a, b):
@@ -262,12 +264,12 @@
 
 
 def joined_fields(displacement, velocity, stiffness, damage):
-    parts = (displacement, velocity, stiffness[None], damage.astype(jnp.float32))
+    parts = (displacement, velocity, stiffness[None], damage)
     total, before = 0.0, 0
     for part in parts:
         count = part.shape[0]
         widths = ((before, FIELD_COUNT - before - count, 0),) + ((0, 0, 0),) * 3
-        total = total + lax.pad(part, jnp.float32(0), widths)
+        total = total + lax.pad(part, part.dtype.type(0), widths).astype(jnp.float32)
         before += count
     return total
 
@@ -277,6 +279,9 @@
     for i, field in enumerate((0, 1, 2, K)):
         for plane in range(3):
             one, two = fields[field, plane + 1], fields[field, plane]
+            if field == K and plane == 0:
+                ((q, _),) = [b for b in BONDS if b[1][0] == 3]
+                one = intact(q, fields[D + q // 11, 1].astype(jnp.int32), one)
             near[3 * i + plane] = jnp.where(even, one, two)
             far[3 * i + plane] = jnp.where(even, two, one)
     for i, (plane, _, word) in enumerate(RIGHT_WORDS):
@@ -510,7 +515,7 @@
     point = f32(3, 4, 8, 128)
     edge = f32(3, 6, 8, 128)
     fields = joined_fields(displacement, velocity, stiffness, damage)
-    far_x, near_x = call(pack_x, [f32(21, 8, 128)] * 2, [], fields)
+    far_x, near_x = call(pack_x, [f32(X_TILES, 8, 128)] * 2, [], fields)
     far_x = swapped(far_x, "gx", 1)
     near_x = swapped(near_x, "gx", 0)
     (force,) = call(first_own, [point], LAYERS, fields, flops=4_000_000)

time: 45.9 us -> 44.9 us (0.978)
  other arithmetic: 1.76 us -> 0.91 us
    convert_element_type x1 -> x0, other arithmetic: 0.9 us -> none  [joined_fields(): damage.astype(jnp.float32)]
where the time goes in v3:
time: 44.9 us; the launch traced here: 44.6 us
  starting transfers between devices  19.2 us (43%)
  waiting for transfers between devices  16.5 us (37%)
  Pallas kernels  7.32 us (16%)
  other arithmetic  0.91 us (2%)
  between operations  0.72 us (2%)
    ppermute x6, starting transfers between devices, swapped(): return lax.ppermute(value, axis, pairs + [(j, i) for i, j in pairs])  19.2 us
    ppermute x6, waiting for transfers between devices, swapped(): return lax.ppermute(value, axis, pairs + [(j, i) for i, j in pairs])  16.5 us
    pallas_call x7, Pallas kernels, call(): pl.pallas_call(kernel, out_shape=outputs, in_specs=[pl.BlockSpec(memory_s...  7.32 us
    add x1, other arithmetic, joined_fields(): total + lax.pad(part, part.dtype.type(0), widths).astype(jnp.float32)  0.91 us
  transfers between devices with their start and end apart: 6, of which 4 were waited for; matrix products, arithmetic and copies ran while one was open for 0% of the time, Pallas kernels for 10%

profile of v3, /device:TPU:384, one launch (start us, length us, event | category | flops | bytes accessed | tf_op | source)
XLA Modules:
  0.0 44.6 jit_solution(11394769548587937728)
XLA Ops:
  0.6 0.9 %convert_add_fusion.fields = f32[13,4,8,128]{3,2,1,0:T(8,128)S(1)} fusion(s32[6,4,8,128]{3,2,1,0:T(8,128)} %param.7, f32[1,4,8,128]{3,2,1,0:T(8,128)} %bitcast.9, f32[3,4,8,128]{3,2,1,0:T(8,128)} %param.5, f32[3,4,8,128]{3,2,1,0:T(8,128)} %param.4), kind=kLoop, calls=%fused_computation | loop fusion | flops 212992 | bytes 425984 | tf_op jit(solution)/shard_map/add | solution.py:272
  1.6 6.3 %collective-permute-start = (f32[20,8,128]{2,1,0:T(8,128)S(1)}, f32[20,8,128]{2,1,0:T(8,128)S(1)}, u32[]{:S(2)}, u32[]{:S(2)}) collective-permute-start(f32[20,8,128]{2,1,0:T(8,128)S(1)} %get-tuple-element.22), channel_id=1, source_target_pairs={{16,32},{48,64},{80,96},{112,128},{144,160},{176,192},{208,224},{2... | collective-permute-start | bytes 245768 | tf_op jit(solution)/shard_map/ppermute | solution.py:511
  7.9 1.9 %collective-permute-start.1 = (f32[20,8,128]{2,1,0:T(8,128)S(1)}, f32[20,8,128]{2,1,0:T(8,128)S(1)}, u32[]{:S(2)}, u32[]{:S(2)}) collective-permute-start(f32[20,8,128]{2,1,0:T(8,128)S(1)} %get-tuple-element.23), channel_id=1, source_target_pairs={{0,16},{32,48},{64,80},{96,112},{128,144},{160,176},{192,208},{224... | collective-permute-start | bytes 245768 | tf_op jit(solution)/shard_map/ppermute | solution.py:511
  9.8 2.1 %shard_map.60.force = f32[3,4,8,128]{3,2,1,0:T(8,128)S(1)} custom-call(f32[13,4,8,128]{3,2,1,0:T(8,128)S(1)} %convert_add_fusion.fields), custom_call_target="tpu_custom_call" | custom-call | flops 4000000 | bytes 4000000 | tf_op jit(solution)/shard_map/pallas_call | solution.py:498
  11.9 0.0 collective-permute-done.far_x
  11.9 2.4 %collective-permute-done.1.near_x = f32[20,8,128]{2,1,0:T(8,128)S(1)} collective-permute-done((f32[20,8,128]{2,1,0:T(8,128)S(1)}, f32[20,8,128]{2,1,0:T(8,128)S(1)}, u32[]{:S(2)}, u32[]{:S(2)}) %collective-permute-start.1) | collective-permute-done | bytes 81952 | tf_op jit(solution)/shard_map/ppermute | solution.py:511
  14.2 0.6 %shard_map.61 = (f32[176,128]{1,0:T(8,128)S(1)}, f32[176,128]{1,0:T(8,128)S(1)}, f32[3,4,8,128]{3,2,1,0:T(8,128)S(1)}) custom-call(f32[13,4,8,128]{3,2,1,0:T(8,128)S(1)} %convert_add_fusion.fields, f32[20,8,128]{2,1,0:T(8,128)S(1)} %collective-permute-done.far_x, f32[20,8,128]{2,1,0:T(8,128)S(1)} %collective-permute-done.1.near_x, ...), custom_call_target="tpu_custom_call" | custom-call | flops 1000 | bytes 1000 | tf_op jit(solution)/shard_map/pallas_call | solution.py:498
  14.8 2.3 %collective-permute-start.2 = (f32[176,128]{1,0:T(8,128)S(1)}, f32[176,128]{1,0:T(8,128)S(1)}, u32[]{:S(2)}, u32[]{:S(2)}) collective-permute-start(f32[176,128]{1,0:T(8,128)S(1)} %get-tuple-element.24), channel_id=1, source_target_pairs={{1,2},{3,4},{5,6},{7,8},{9,10},{11,12},{13,14},{2,1},{4,3},{6,5},{... | collective-permute-start | bytes 270344 | tf_op jit(solution)/shard_map/ppermute | solution.py:511
  17.1 3.2 %collective-permute-start.3 = (f32[176,128]{1,0:T(8,128)S(1)}, f32[176,128]{1,0:T(8,128)S(1)}, u32[]{:S(2)}, u32[]{:S(2)}) collective-permute-start(f32[176,128]{1,0:T(8,128)S(1)} %get-tuple-element.25), channel_id=1, source_target_pairs={{0,1},{2,3},{4,5},{6,7},{8,9},{10,11},{12,13},{14,15},{1,0},{3,2},... | collective-permute-start | bytes 270344 | tf_op jit(solution)/shard_map/ppermute | solution.py:511
  20.3 0.4 shard_map.62
  20.7 12.3 %collective-permute-done.2.b = f32[176,128]{1,0:T(8,128)S(1)} collective-permute-done((f32[176,128]{1,0:T(8,128)S(1)}, f32[176,128]{1,0:T(8,128)S(1)}, u32[]{:S(2)}, u32[]{:S(2)}) %collective-permute-start.2) | collective-permute-done | bytes 90144 | tf_op jit(solution)/shard_map/ppermute | solution.py:511
  33.0 0.0 collective-permute-done.3.a
  33.0 1.0 %shard_map.63 = (f32[3,4,8,128]{3,2,1,0:T(8,128)S(1)}, f32[3,4,8,128]{3,2,1,0:T(8,128)S(1)}, f32[3,6,8,128]{3,2,1,0:T(8,128)S(1)}, f32[96,128]{1,0:T(8,128)S(1)}, f32[96,128]{1,0:T(8,128)S(1)}) custom-call(f32[13,4,8,128]{3,2,1,0:T(8,128)S(1)} %convert_add_fusion.fields, f32[176,128]{1,0:T(8,128)S(1)} %collective-permute-done.2.b, ...), custom_call_target="tpu_custom_call" | custom-call | flops 1000 | bytes 1000 | tf_op jit(solution)/shard_map/pallas_call | solution.py:498
  33.9 3.5 %collective-permute-start.4 = (f32[12,8,128]{2,1,0:T(8,128)S(1)}, f32[12,8,128]{2,1,0:T(8,128)S(1)}, u32[]{:S(2)}, u32[]{:S(2)}) collective-permute-start(f32[12,8,128]{2,1,0:T(8,128)S(1)} %bitcast.8), channel_id=1, source_target_pairs={{16,32},{48,64},{80,96},{112,128},{144,160},{176,192},{208,224},{2... | collective-permute-start | bytes 147464 | tf_op jit(solution)/shard_map/ppermute | solution.py:511
  37.5 1.9 %collective-permute-start.5 = (f32[12,8,128]{2,1,0:T(8,128)S(1)}, f32[12,8,128]{2,1,0:T(8,128)S(1)}, u32[]{:S(2)}, u32[]{:S(2)}) collective-permute-start(f32[12,8,128]{2,1,0:T(8,128)S(1)} %bitcast.7), channel_id=1, source_target_pairs={{0,16},{32,48},{64,80},{96,112},{128,144},{160,176},{192,208},{224... | collective-permute-start | bytes 147464 | tf_op jit(solution)/shard_map/ppermute | solution.py:511
  39.4 2.2 %shard_map.64 = (f32[3,4,8,128]{3,2,1,0:T(8,128)S(1)}, f32[10,16,128]{2,1,0:T(8,128)S(1)}, f32[4,10,16,128]{3,2,1,0:T(8,128)S(1)}, s32[6,10,16,128]{3,2,1,0:T(8,128)S(1)}) custom-call(f32[13,4,8,128]{3,2,1,0:T(8,128)S(1)} %convert_add_fusion.fields, f32[20,8,128]{2,1,0:T(8,128)S(1)} %collective-permute-done.far_x, ...), custom_call_target="tpu_custom_call" | custom-call | flops 4000000 | bytes 4000000 | tf_op jit(solution)/shard_map/pallas_call | solution.py:498
  41.6 1.6 %collective-permute-done.4 = f32[12,8,128]{2,1,0:T(8,128)S(1)} collective-permute-done((f32[12,8,128]{2,1,0:T(8,128)S(1)}, f32[12,8,128]{2,1,0:T(8,128)S(1)}, u32[]{:S(2)}, u32[]{:S(2)}) %collective-permute-start.4) | collective-permute-done | bytes 49184 | tf_op jit(solution)/shard_map/ppermute | solution.py:511
  43.2 0.2 collective-permute-done.5
  43.5 1.2 %shard_map.65 = (f32[3,4,8,128]{3,2,1,0:T(8,128)}, f32[3,4,8,128]{3,2,1,0:T(8,128)}) custom-call(f32[3,4,8,128]{3,2,1,0:T(8,128)S(1)} %get-tuple-element.33.near, f32[3,4,8,128]{3,2,1,0:T(8,128)S(1)} %get-tuple-element.34.v_in, f32[3,4,8,128]{3,2,1,0:T(8,128)S(1)} %get-tuple-element.36.force, f32[10,16,128]{2,1,0:T(8,128)S(1)} %get-tuple-element.37.s, ...), custom_call_target="tpu_custom_call" | custom-call | flops 1000 | bytes 1000 | tf_op jit(solution)/shard_map/pallas_call | solution.py:498
  (1 shorter events, 0.0 us)
Async XLA Ops:
  1.6 10.3 %collective-permute-start = (f32[20,8,128]{2,1,0:T(8,128)S(1)}, f32[20,8,128]{2,1,0:T(8,128)S(1)}, u32[]{:S(2)}, u32[]{:S(2)}) collective-permute-start(f32[20,8,128]{2,1,0:T(8,128)S(1)} %get-tuple-element.22), channel_id=1, source_target_pairs={{16,32},{48,64},{80,96},{112,128},{144,160},{176,192},{208,224},{2... | collective-permute-start | bytes 245768 | tf_op jit(solution)/shard_map/ppermute | solution.py:511
  7.9 6.3 %collective-permute-start.1 = (f32[20,8,128]{2,1,0:T(8,128)S(1)}, f32[20,8,128]{2,1,0:T(8,128)S(1)}, u32[]{:S(2)}, u32[]{:S(2)}) collective-permute-start(f32[20,8,128]{2,1,0:T(8,128)S(1)} %get-tuple-element.23), channel_id=1, source_target_pairs={{0,16},{32,48},{64,80},{96,112},{128,144},{160,176},{192,208},{224... | collective-permute-start | bytes 245768 | tf_op jit(solution)/shard_map/ppermute | solution.py:511
  14.8 18.1 %collective-permute-start.2 = (f32[176,128]{1,0:T(8,128)S(1)}, f32[176,128]{1,0:T(8,128)S(1)}, u32[]{:S(2)}, u32[]{:S(2)}) collective-permute-start(f32[176,128]{1,0:T(8,128)S(1)} %get-tuple-element.24), channel_id=1, source_target_pairs={{1,2},{3,4},{5,6},{7,8},{9,10},{11,12},{13,14},{2,1},{4,3},{6,5},{... | collective-permute-start | bytes 270344 | tf_op jit(solution)/shard_map/ppermute | solution.py:511
  17.1 15.9 %collective-permute-start.3 = (f32[176,128]{1,0:T(8,128)S(1)}, f32[176,128]{1,0:T(8,128)S(1)}, u32[]{:S(2)}, u32[]{:S(2)}) collective-permute-start(f32[176,128]{1,0:T(8,128)S(1)} %get-tuple-element.25), channel_id=1, source_target_pairs={{0,1},{2,3},{4,5},{6,7},{8,9},{10,11},{12,13},{14,15},{1,0},{3,2},... | collective-permute-start | bytes 270344 | tf_op jit(solution)/shard_map/ppermute | solution.py:511
  33.9 9.3 %collective-permute-start.4 = (f32[12,8,128]{2,1,0:T(8,128)S(1)}, f32[12,8,128]{2,1,0:T(8,128)S(1)}, u32[]{:S(2)}, u32[]{:S(2)}) collective-permute-start(f32[12,8,128]{2,1,0:T(8,128)S(1)} %bitcast.8), channel_id=1, source_target_pairs={{16,32},{48,64},{80,96},{112,128},{144,160},{176,192},{208,224},{2... | collective-permute-start | bytes 147464 | tf_op jit(solution)/shard_map/ppermute | solution.py:511
  37.5 6.0 %collective-permute-start.5 = (f32[12,8,128]{2,1,0:T(8,128)S(1)}, f32[12,8,128]{2,1,0:T(8,128)S(1)}, u32[]{:S(2)}, u32[]{:S(2)}) collective-permute-start(f32[12,8,128]{2,1,0:T(8,128)S(1)} %bitcast.7), channel_id=1, source_target_pairs={{0,16},{32,48},{64,80},{96,112},{128,144},{160,176},{192,208},{224... | collective-permute-start | bytes 147464 | tf_op jit(solution)/shard_map/ppermute | solution.py:511

commit v4 on v3

--- a/solution.py
+++ b/solution.py
@@ -333,8 +333,11 @@
         put_zeros(s, [()], SIDES, row, count)
     put_own(fields, u, s, d)
     put_sides(even_x, near_x, far_x, u, s, d)
-    roll_field(u, ur, (7, 8))
-    roll_stiffness(s, sr, (7, 8))
+    for row, count in OUTER:
+        put_zeros(ur, [(c, i) for c in range(3) for i in range(4)], (7, 8), row, count)
+        put_zeros(sr, [(i,) for i in range(4)], (7, 8), row, count)
+    roll_field(u, ur, (7, 8), (LOW,))
+    roll_stiffness(s, sr, (7, 8), (LOW,))
     for x in range(4):
         total = side_part(x, u, ur, s, sr, d)
         scale = bond_scale * s[spot(s, x + 3, LOW)]
@@ -361,6 +364,8 @@
 
 def roll_lines(u, ur, s, sr, d, dr, words):
     for at in range(6):
+        if not words[at]:
+            continue
         for i, ez in enumerate(ROLLS):
             for w in words[at]:
                 dr[w, i, at, 0:8] = rolled(d[w, at, 0:8], ez)
@@ -388,6 +393,7 @@
     put_lines(even, a, b, hu, hs, hd, edge)
     sent = UP_SLOTS + DOWN_SLOTS
     words = [[k[1] for k in sent if k[0] == "w" and line_of(k[3]) == at] for at in range(6)]
+    words[0] = words[5] = []
     roll_lines(hu, hur, hs, hsr, hd, hdr, words)
     beside = (u, ur, s, sr, d, dr)
     beyond = (hu, hur, hs, hsr, hd, hdr)

time: 44.9 us -> 44.9 us (level)
  no operation moved by 1% of the time
where the time goes in v4:
time: 44.9 us; the launch traced here: 44.6 us
  starting transfers between devices  19.2 us (43%)
  waiting for transfers between devices  16.5 us (37%)
  Pallas kernels  7.3 us (16%)
  other arithmetic  0.91 us (2%)
  between operations  0.72 us (2%)
    ppermute x6, starting transfers between devices, swapped(): return lax.ppermute(value, axis, pairs + [(j, i) for i, j in pairs])  19.2 us
    ppermute x6, waiting for transfers between devices, swapped(): return lax.ppermute(value, axis, pairs + [(j, i) for i, j in pairs])  16.5 us
    pallas_call x7, Pallas kernels, call(): pl.pallas_call(kernel, out_shape=outputs, in_specs=[pl.BlockSpec(memory_s...  7.3 us
    add x1, other arithmetic, joined_fields(): total + lax.pad(part, part.dtype.type(0), widths).astype(jnp.float32)  0.91 us
  transfers between devices with their start and end apart: 6, of which 4 were waited for; matrix products, arithmetic and copies ran while one was open for 0% of the time, Pallas kernels for 10%

profile of v4, /device:TPU:384, one launch (start us, length us, event | category | flops | bytes accessed | tf_op | source)
XLA Modules:
  0.0 44.6 jit_solution(6548427927299803829)
XLA Ops:
  0.6 0.9 %convert_add_fusion.fields = f32[13,4,8,128]{3,2,1,0:T(8,128)S(1)} fusion(s32[6,4,8,128]{3,2,1,0:T(8,128)} %param.7, f32[1,4,8,128]{3,2,1,0:T(8,128)} %bitcast.9, f32[3,4,8,128]{3,2,1,0:T(8,128)} %param.5, f32[3,4,8,128]{3,2,1,0:T(8,128)} %param.4), kind=kLoop, calls=%fused_computation | loop fusion | flops 212992 | bytes 425984 | tf_op jit(solution)/shard_map/add | solution.py:272
  1.6 6.3 %collective-permute-start = (f32[20,8,128]{2,1,0:T(8,128)S(1)}, f32[20,8,128]{2,1,0:T(8,128)S(1)}, u32[]{:S(2)}, u32[]{:S(2)}) collective-permute-start(f32[20,8,128]{2,1,0:T(8,128)S(1)} %get-tuple-element.22), channel_id=1, source_target_pairs={{16,32},{48,64},{80,96},{112,128},{144,160},{176,192},{208,224},{2... | collective-permute-start | bytes 245768 | tf_op jit(solution)/shard_map/ppermute | solution.py:517
  7.9 1.9 %collective-permute-start.1 = (f32[20,8,128]{2,1,0:T(8,128)S(1)}, f32[20,8,128]{2,1,0:T(8,128)S(1)}, u32[]{:S(2)}, u32[]{:S(2)}) collective-permute-start(f32[20,8,128]{2,1,0:T(8,128)S(1)} %get-tuple-element.23), channel_id=1, source_target_pairs={{0,16},{32,48},{64,80},{96,112},{128,144},{160,176},{192,208},{224... | collective-permute-start | bytes 245768 | tf_op jit(solution)/shard_map/ppermute | solution.py:517
  9.8 2.1 %shard_map.60.force = f32[3,4,8,128]{3,2,1,0:T(8,128)S(1)} custom-call(f32[13,4,8,128]{3,2,1,0:T(8,128)S(1)} %convert_add_fusion.fields), custom_call_target="tpu_custom_call" | custom-call | flops 4000000 | bytes 4000000 | tf_op jit(solution)/shard_map/pallas_call | solution.py:504
  11.9 0.0 collective-permute-done.far_x
  11.9 2.4 %collective-permute-done.1.near_x = f32[20,8,128]{2,1,0:T(8,128)S(1)} collective-permute-done((f32[20,8,128]{2,1,0:T(8,128)S(1)}, f32[20,8,128]{2,1,0:T(8,128)S(1)}, u32[]{:S(2)}, u32[]{:S(2)}) %collective-permute-start.1) | collective-permute-done | bytes 81952 | tf_op jit(solution)/shard_map/ppermute | solution.py:517
  14.2 0.6 %shard_map.61 = (f32[176,128]{1,0:T(8,128)S(1)}, f32[176,128]{1,0:T(8,128)S(1)}, f32[3,4,8,128]{3,2,1,0:T(8,128)S(1)}) custom-call(f32[13,4,8,128]{3,2,1,0:T(8,128)S(1)} %convert_add_fusion.fields, f32[20,8,128]{2,1,0:T(8,128)S(1)} %collective-permute-done.far_x, f32[20,8,128]{2,1,0:T(8,128)S(1)} %collective-permute-done.1.near_x, ...), custom_call_target="tpu_custom_call" | custom-call | flops 1000 | bytes 1000 | tf_op jit(solution)/shard_map/pallas_call | solution.py:504
  14.8 2.3 %collective-permute-start.2 = (f32[176,128]{1,0:T(8,128)S(1)}, f32[176,128]{1,0:T(8,128)S(1)}, u32[]{:S(2)}, u32[]{:S(2)}) collective-permute-start(f32[176,128]{1,0:T(8,128)S(1)} %get-tuple-element.24), channel_id=1, source_target_pairs={{1,2},{3,4},{5,6},{7,8},{9,10},{11,12},{13,14},{2,1},{4,3},{6,5},{... | collective-permute-start | bytes 270344 | tf_op jit(solution)/shard_map/ppermute | solution.py:517
  17.1 3.2 %collective-permute-start.3 = (f32[176,128]{1,0:T(8,128)S(1)}, f32[176,128]{1,0:T(8,128)S(1)}, u32[]{:S(2)}, u32[]{:S(2)}) collective-permute-start(f32[176,128]{1,0:T(8,128)S(1)} %get-tuple-element.25), channel_id=1, source_target_pairs={{0,1},{2,3},{4,5},{6,7},{8,9},{10,11},{12,13},{14,15},{1,0},{3,2},... | collective-permute-start | bytes 270344 | tf_op jit(solution)/shard_map/ppermute | solution.py:517
  20.4 0.4 shard_map.62
  20.7 12.3 %collective-permute-done.2.b = f32[176,128]{1,0:T(8,128)S(1)} collective-permute-done((f32[176,128]{1,0:T(8,128)S(1)}, f32[176,128]{1,0:T(8,128)S(1)}, u32[]{:S(2)}, u32[]{:S(2)}) %collective-permute-start.2) | collective-permute-done | bytes 90144 | tf_op jit(solution)/shard_map/ppermute | solution.py:517
  33.0 0.0 collective-permute-done.3.a
  33.0 0.9 %shard_map.63 = (f32[3,4,8,128]{3,2,1,0:T(8,128)S(1)}, f32[3,4,8,128]{3,2,1,0:T(8,128)S(1)}, f32[3,6,8,128]{3,2,1,0:T(8,128)S(1)}, f32[96,128]{1,0:T(8,128)S(1)}, f32[96,128]{1,0:T(8,128)S(1)}) custom-call(f32[13,4,8,128]{3,2,1,0:T(8,128)S(1)} %convert_add_fusion.fields, f32[176,128]{1,0:T(8,128)S(1)} %collective-permute-done.2.b, ...), custom_call_target="tpu_custom_call" | custom-call | flops 1000 | bytes 1000 | tf_op jit(solution)/shard_map/pallas_call | solution.py:504
  33.9 3.5 %collective-permute-start.4 = (f32[12,8,128]{2,1,0:T(8,128)S(1)}, f32[12,8,128]{2,1,0:T(8,128)S(1)}, u32[]{:S(2)}, u32[]{:S(2)}) collective-permute-start(f32[12,8,128]{2,1,0:T(8,128)S(1)} %bitcast.8), channel_id=1, source_target_pairs={{16,32},{48,64},{80,96},{112,128},{144,160},{176,192},{208,224},{2... | collective-permute-start | bytes 147464 | tf_op jit(solution)/shard_map/ppermute | solution.py:517
  37.5 1.9 %collective-permute-start.5 = (f32[12,8,128]{2,1,0:T(8,128)S(1)}, f32[12,8,128]{2,1,0:T(8,128)S(1)}, u32[]{:S(2)}, u32[]{:S(2)}) collective-permute-start(f32[12,8,128]{2,1,0:T(8,128)S(1)} %bitcast.7), channel_id=1, source_target_pairs={{0,16},{32,48},{64,80},{96,112},{128,144},{160,176},{192,208},{224... | collective-permute-start | bytes 147464 | tf_op jit(solution)/shard_map/ppermute | solution.py:517
  39.4 2.2 %shard_map.64 = (f32[3,4,8,128]{3,2,1,0:T(8,128)S(1)}, f32[10,16,128]{2,1,0:T(8,128)S(1)}, f32[4,10,16,128]{3,2,1,0:T(8,128)S(1)}, s32[6,10,16,128]{3,2,1,0:T(8,128)S(1)}) custom-call(f32[13,4,8,128]{3,2,1,0:T(8,128)S(1)} %convert_add_fusion.fields, f32[20,8,128]{2,1,0:T(8,128)S(1)} %collective-permute-done.far_x, ...), custom_call_target="tpu_custom_call" | custom-call | flops 4000000 | bytes 4000000 | tf_op jit(solution)/shard_map/pallas_call | solution.py:504
  41.6 1.6 %collective-permute-done.4 = f32[12,8,128]{2,1,0:T(8,128)S(1)} collective-permute-done((f32[12,8,128]{2,1,0:T(8,128)S(1)}, f32[12,8,128]{2,1,0:T(8,128)S(1)}, u32[]{:S(2)}, u32[]{:S(2)}) %collective-permute-start.4) | collective-permute-done | bytes 49184 | tf_op jit(solution)/shard_map/ppermute | solution.py:517
  43.2 0.2 collective-permute-done.5
  43.4 1.2 %shard_map.65 = (f32[3,4,8,128]{3,2,1,0:T(8,128)}, f32[3,4,8,128]{3,2,1,0:T(8,128)}) custom-call(f32[3,4,8,128]{3,2,1,0:T(8,128)S(1)} %get-tuple-element.33.near, f32[3,4,8,128]{3,2,1,0:T(8,128)S(1)} %get-tuple-element.34.v_in, f32[3,4,8,128]{3,2,1,0:T(8,128)S(1)} %get-tuple-element.36.force, f32[10,16,128]{2,1,0:T(8,128)S(1)} %get-tuple-element.37.s, ...), custom_call_target="tpu_custom_call" | custom-call | flops 1000 | bytes 1000 | tf_op jit(solution)/shard_map/pallas_call | solution.py:504
  (1 shorter events, 0.0 us)
Async XLA Ops:
  1.6 10.3 %collective-permute-start = (f32[20,8,128]{2,1,0:T(8,128)S(1)}, f32[20,8,128]{2,1,0:T(8,128)S(1)}, u32[]{:S(2)}, u32[]{:S(2)}) collective-permute-start(f32[20,8,128]{2,1,0:T(8,128)S(1)} %get-tuple-element.22), channel_id=1, source_target_pairs={{16,32},{48,64},{80,96},{112,128},{144,160},{176,192},{208,224},{2... | collective-permute-start | bytes 245768 | tf_op jit(solution)/shard_map/ppermute | solution.py:517
  7.9 6.3 %collective-permute-start.1 = (f32[20,8,128]{2,1,0:T(8,128)S(1)}, f32[20,8,128]{2,1,0:T(8,128)S(1)}, u32[]{:S(2)}, u32[]{:S(2)}) collective-permute-start(f32[20,8,128]{2,1,0:T(8,128)S(1)} %get-tuple-element.23), channel_id=1, source_target_pairs={{0,16},{32,48},{64,80},{96,112},{128,144},{160,176},{192,208},{224... | collective-permute-start | bytes 245768 | tf_op jit(solution)/shard_map/ppermute | solution.py:517
  14.8 18.1 %collective-permute-start.2 = (f32[176,128]{1,0:T(8,128)S(1)}, f32[176,128]{1,0:T(8,128)S(1)}, u32[]{:S(2)}, u32[]{:S(2)}) collective-permute-start(f32[176,128]{1,0:T(8,128)S(1)} %get-tuple-element.24), channel_id=1, source_target_pairs={{1,2},{3,4},{5,6},{7,8},{9,10},{11,12},{13,14},{2,1},{4,3},{6,5},{... | collective-permute-start | bytes 270344 | tf_op jit(solution)/shard_map/ppermute | solution.py:517
  17.1 15.9 %collective-permute-start.3 = (f32[176,128]{1,0:T(8,128)S(1)}, f32[176,128]{1,0:T(8,128)S(1)}, u32[]{:S(2)}, u32[]{:S(2)}) collective-permute-start(f32[176,128]{1,0:T(8,128)S(1)} %get-tuple-element.25), channel_id=1, source_target_pairs={{0,1},{2,3},{4,5},{6,7},{8,9},{10,11},{12,13},{14,15},{1,0},{3,2},... | collective-permute-start | bytes 270344 | tf_op jit(solution)/shard_map/ppermute | solution.py:517
  33.9 9.3 %collective-permute-start.4 = (f32[12,8,128]{2,1,0:T(8,128)S(1)}, f32[12,8,128]{2,1,0:T(8,128)S(1)}, u32[]{:S(2)}, u32[]{:S(2)}) collective-permute-start(f32[12,8,128]{2,1,0:T(8,128)S(1)} %bitcast.8), channel_id=1, source_target_pairs={{16,32},{48,64},{80,96},{112,128},{144,160},{176,192},{208,224},{2... | collective-permute-start | bytes 147464 | tf_op jit(solution)/shard_map/ppermute | solution.py:517
  37.5 6.0 %collective-permute-start.5 = (f32[12,8,128]{2,1,0:T(8,128)S(1)}, f32[12,8,128]{2,1,0:T(8,128)S(1)}, u32[]{:S(2)}, u32[]{:S(2)}) collective-permute-start(f32[12,8,128]{2,1,0:T(8,128)S(1)} %bitcast.7), channel_id=1, source_target_pairs={{0,16},{32,48},{64,80},{96,112},{128,144},{160,176},{192,208},{224... | collective-permute-start | bytes 147464 | tf_op jit(solution)/shard_map/ppermute | solution.py:517

commit v5 on v4

--- a/solution.py
+++ b/solution.py
@@ -14,7 +14,7 @@
 
 PLANES, ROWS = 10, 16
 LOW = 3
-V, K, D, FIELD_COUNT = 3, 6, 7, 13
+K, D, FIELD_COUNT = 3, 4, 10
 ROLLS = (-2, -1, 1, 2)
 
 
@@ -263,8 +263,8 @@
     return tuple(lax.axis_index(axis) % 2 == 0 for axis in ("gx", "gy"))
 
 
-def joined_fields(displacement, velocity, stiffness, damage):
-    parts = (displacement, velocity, stiffness[None], damage)
+def joined_fields(displacement, stiffness, damage):
+    parts = (displacement, stiffness[None], damage)
     total, before = 0.0, 0
     for part in parts:
         count = part.shape[0]
@@ -315,7 +315,8 @@
     return accumulate(x + 3, LOW, owned, reacted, u, ur, s, sr, d)
 
 
-def first_own(fields, force, u, ur, s, sr, d):
+def first_own(fields, v_in, force, v_kept, u, ur, s, sr, d):
+    v_kept[...] = v_in[...]
     put_zeros(u, EACH, SIDES, 0, ROWS)
     put_zeros(s, [()], SIDES, 0, ROWS)
     for row, count in OUTER:
@@ -326,7 +327,7 @@
     own_part(u, ur, s, sr, d, force)
 
 
-def first_sides(fields, far_x, near_x, force, b, a, v_part, u, ur, s, sr, d, near, up, down):
+def first_sides(fields, v_in, far_x, near_x, force, b, a, v_part, u, ur, s, sr, d, near, up, down):
     even_x, even = even_place()
     for row, count in OUTER:
         put_zeros(u, EACH, SIDES, row, count)
@@ -342,7 +343,7 @@
         total = side_part(x, u, ur, s, sr, d)
         scale = bond_scale * s[spot(s, x + 3, LOW)]
         for c in range(3):
-            velocity = fields[V + c, x] + time_step * (scale * (force[c, x] + total[c]))
+            velocity = v_in[c, x] + time_step * (scale * (force[c, x] + total[c]))
             v_part[c, x] = velocity
             near[(c,) + spot(u, x + 3, LOW)] = fields[c, x] + time_step * velocity
 
@@ -520,14 +521,14 @@
 def shards(displacement, velocity, stiffness, damage):
     point = f32(3, 4, 8, 128)
     edge = f32(3, 6, 8, 128)
-    fields = joined_fields(displacement, velocity, stiffness, damage)
+    fields = joined_fields(displacement, stiffness, damage)
     far_x, near_x = call(pack_x, [f32(X_TILES, 8, 128)] * 2, [], fields)
     far_x = swapped(far_x, "gx", 1)
     near_x = swapped(near_x, "gx", 0)
-    (force,) = call(first_own, [point], LAYERS, fields, flops=4_000_000)
+    force, velocity = call(first_own, [point, point], LAYERS, fields, velocity, flops=4_000_000)
     message = f32(Y_ROWS, 128)
     b, a, v_part = call(
-        first_sides, [message, message, point], FLAT + [FLAT[0], message, message], fields, far_x, near_x, force
+        first_sides, [message, message, point], FLAT + [FLAT[0], message, message], fields, velocity, far_x, near_x, force
     )
     b = swapped(b, "gy", 1)
     a = swapped(a, "gy", 0)

time: 44.9 us -> 45.2 us (level)
  local copies, waits for them, and re-layouts: 0 us -> 0.79 us
    unnamed x0 -> x2, local copies, waits for them, and re-layouts: none -> 0.79 us
  transfers between devices with their start and end apart: 6 -> 6, of which waited for: 4 -> 3; matrix products, arithmetic and copies ran while one was open for 0% -> 0% of each run, Pallas kernels for 10% -> 10%
where the time goes in v5:
time: 45.2 us; the launch traced here: 44.9 us
  starting transfers between devices  19 us (42%)
  waiting for transfers between devices  16.2 us (36%)
  Pallas kernels  7.25 us (16%)
  other arithmetic  0.93 us (2%)
  local copies, waits for them, and re-layouts  0.79 us (2%)
  between operations  0.72 us (2%)
    ppermute x6, starting transfers between devices, swapped(): return lax.ppermute(value, axis, pairs + [(j, i) for i, j in pairs])  19 us
    ppermute x6, waiting for transfers between devices, swapped(): return lax.ppermute(value, axis, pairs + [(j, i) for i, j in pairs])  16.2 us
    pallas_call x7, Pallas kernels, call(): pl.pallas_call(kernel, out_shape=outputs, in_specs=[pl.BlockSpec(memory_s...  7.25 us
    add x1, other arithmetic, joined_fields(): total + lax.pad(part, part.dtype.type(0), widths).astype(jnp.float32)  0.93 us
  transfers between devices with their start and end apart: 6, of which 3 were waited for; matrix products, arithmetic and copies ran while one was open for 0% of the time, Pallas kernels for 10%

profile of v5, /device:TPU:384, one launch (start us, length us, event | category | flops | bytes accessed | tf_op | source)
XLA Modules:
  0.0 44.9 jit_solution(17639254837684856167)
XLA Ops:
  0.6 0.9 %convert_add_fusion.fields = f32[10,4,8,128]{3,2,1,0:T(8,128)S(1)} fusion(s32[6,4,8,128]{3,2,1,0:T(8,128)} %param.7, f32[1,4,8,128]{3,2,1,0:T(8,128)} %bitcast.9, f32[3,4,8,128]{3,2,1,0:T(8,128)} %param.4), kind=kLoop, calls=%fused_computation | loop fusion | flops 122880 | bytes 327680 | tf_op jit(solution)/shard_map/add | solution.py:272
  1.6 6.3 %collective-permute-start = (f32[20,8,128]{2,1,0:T(8,128)S(1)}, f32[20,8,128]{2,1,0:T(8,128)S(1)}, u32[]{:S(2)}, u32[]{:S(2)}) collective-permute-start(f32[20,8,128]{2,1,0:T(8,128)S(1)} %get-tuple-element.25), channel_id=1, source_target_pairs={{16,32},{48,64},{80,96},{112,128},{144,160},{176,192},{208,224},{2... | collective-permute-start | bytes 245768 | tf_op jit(solution)/shard_map/ppermute | solution.py:518
  7.9 1.9 %collective-permute-start.1 = (f32[20,8,128]{2,1,0:T(8,128)S(1)}, f32[20,8,128]{2,1,0:T(8,128)S(1)}, u32[]{:S(2)}, u32[]{:S(2)}) collective-permute-start(f32[20,8,128]{2,1,0:T(8,128)S(1)} %get-tuple-element.26), channel_id=1, source_target_pairs={{0,16},{32,48},{64,80},{96,112},{128,144},{160,176},{192,208},{224... | collective-permute-start | bytes 245768 | tf_op jit(solution)/shard_map/ppermute | solution.py:518
  9.8 0.0 copy-start
  9.9 0.8 %copy-done = f32[3,4,8,128]{3,2,1,0:T(8,128)S(1)} copy-done((f32[3,4,8,128]{3,2,1,0:T(8,128)S(1)}, f32[3,4,8,128]{3,2,1,0:T(8,128)}, u32[]{:S(2)}) %copy-start) | copy-done | bytes 49176
  10.7 2.1 %shard_map.59 = (f32[3,4,8,128]{3,2,1,0:T(8,128)S(1)}, f32[3,4,8,128]{3,2,1,0:T(8,128)S(1)}) custom-call(f32[10,4,8,128]{3,2,1,0:T(8,128)S(1)} %convert_add_fusion.fields, f32[3,4,8,128]{3,2,1,0:T(8,128)S(1)} %copy-done), custom_call_target="tpu_custom_call" | custom-call | flops 4000000 | bytes 4000000 | tf_op jit(solution)/shard_map/pallas_call | solution.py:505
  12.7 0.0 collective-permute-done.far_x
  12.7 1.5 %collective-permute-done.1.near_x = f32[20,8,128]{2,1,0:T(8,128)S(1)} collective-permute-done((f32[20,8,128]{2,1,0:T(8,128)S(1)}, f32[20,8,128]{2,1,0:T(8,128)S(1)}, u32[]{:S(2)}, u32[]{:S(2)}) %collective-permute-start.1) | collective-permute-done | bytes 81952 | tf_op jit(solution)/shard_map/ppermute | solution.py:518
  14.3 0.6 %shard_map.61 = (f32[176,128]{1,0:T(8,128)S(1)}, f32[176,128]{1,0:T(8,128)S(1)}, f32[3,4,8,128]{3,2,1,0:T(8,128)S(1)}) custom-call(f32[10,4,8,128]{3,2,1,0:T(8,128)S(1)} %convert_add_fusion.fields, f32[3,4,8,128]{3,2,1,0:T(8,128)S(1)} %get-tuple-element.24.v_in, f32[20,8,128]{2,1,0:T(8,128)S(1)} %collective-permute-done.far_x, ...), custom_call_target="tpu_custom_call" | custom-call | flops 1000 | bytes 1000 | tf_op jit(solution)/shard_map/pallas_call | solution.py:505
  14.8 2.3 %collective-permute-start.2 = (f32[176,128]{1,0:T(8,128)S(1)}, f32[176,128]{1,0:T(8,128)S(1)}, u32[]{:S(2)}, u32[]{:S(2)}) collective-permute-start(f32[176,128]{1,0:T(8,128)S(1)} %get-tuple-element.28), channel_id=1, source_target_pairs={{1,2},{3,4},{5,6},{7,8},{9,10},{11,12},{13,14},{2,1},{4,3},{6,5},{... | collective-permute-start | bytes 270344 | tf_op jit(solution)/shard_map/ppermute | solution.py:518
  17.1 3.2 %collective-permute-start.3 = (f32[176,128]{1,0:T(8,128)S(1)}, f32[176,128]{1,0:T(8,128)S(1)}, u32[]{:S(2)}, u32[]{:S(2)}) collective-permute-start(f32[176,128]{1,0:T(8,128)S(1)} %get-tuple-element.29), channel_id=1, source_target_pairs={{0,1},{2,3},{4,5},{6,7},{8,9},{10,11},{12,13},{14,15},{1,0},{3,2},... | collective-permute-start | bytes 270344 | tf_op jit(solution)/shard_map/ppermute | solution.py:518
  20.4 0.4 shard_map.62
  20.7 12.7 %collective-permute-done.2.b = f32[176,128]{1,0:T(8,128)S(1)} collective-permute-done((f32[176,128]{1,0:T(8,128)S(1)}, f32[176,128]{1,0:T(8,128)S(1)}, u32[]{:S(2)}, u32[]{:S(2)}) %collective-permute-start.2) | collective-permute-done | bytes 90144 | tf_op jit(solution)/shard_map/ppermute | solution.py:518
  33.4 0.0 collective-permute-done.3.a
  33.4 0.9 %shard_map.63 = (f32[3,4,8,128]{3,2,1,0:T(8,128)S(1)}, f32[3,4,8,128]{3,2,1,0:T(8,128)S(1)}, f32[3,6,8,128]{3,2,1,0:T(8,128)S(1)}, f32[96,128]{1,0:T(8,128)S(1)}, f32[96,128]{1,0:T(8,128)S(1)}) custom-call(f32[10,4,8,128]{3,2,1,0:T(8,128)S(1)} %convert_add_fusion.fields, f32[176,128]{1,0:T(8,128)S(1)} %collective-permute-done.2.b, ...), custom_call_target="tpu_custom_call" | custom-call | flops 1000 | bytes 1000 | tf_op jit(solution)/shard_map/pallas_call | solution.py:505
  34.4 3.3 %collective-permute-start.4 = (f32[12,8,128]{2,1,0:T(8,128)S(1)}, f32[12,8,128]{2,1,0:T(8,128)S(1)}, u32[]{:S(2)}, u32[]{:S(2)}) collective-permute-start(f32[12,8,128]{2,1,0:T(8,128)S(1)} %bitcast.8), channel_id=1, source_target_pairs={{16,32},{48,64},{80,96},{112,128},{144,160},{176,192},{208,224},{2... | collective-permute-start | bytes 147464 | tf_op jit(solution)/shard_map/ppermute | solution.py:518
  37.7 1.9 %collective-permute-start.5 = (f32[12,8,128]{2,1,0:T(8,128)S(1)}, f32[12,8,128]{2,1,0:T(8,128)S(1)}, u32[]{:S(2)}, u32[]{:S(2)}) collective-permute-start(f32[12,8,128]{2,1,0:T(8,128)S(1)} %bitcast.7), channel_id=1, source_target_pairs={{0,16},{32,48},{64,80},{96,112},{128,144},{160,176},{192,208},{224... | collective-permute-start | bytes 147464 | tf_op jit(solution)/shard_map/ppermute | solution.py:518
  39.6 2.1 %shard_map.64 = (f32[3,4,8,128]{3,2,1,0:T(8,128)S(1)}, f32[10,16,128]{2,1,0:T(8,128)S(1)}, f32[4,10,16,128]{3,2,1,0:T(8,128)S(1)}, s32[6,10,16,128]{3,2,1,0:T(8,128)S(1)}) custom-call(f32[10,4,8,128]{3,2,1,0:T(8,128)S(1)} %convert_add_fusion.fields, f32[20,8,128]{2,1,0:T(8,128)S(1)} %collective-permute-done.far_x, ...), custom_call_target="tpu_custom_call" | custom-call | flops 4000000 | bytes 4000000 | tf_op jit(solution)/shard_map/pallas_call | solution.py:505
  41.8 1.9 %collective-permute-done.4 = f32[12,8,128]{2,1,0:T(8,128)S(1)} collective-permute-done((f32[12,8,128]{2,1,0:T(8,128)S(1)}, f32[12,8,128]{2,1,0:T(8,128)S(1)}, u32[]{:S(2)}, u32[]{:S(2)}) %collective-permute-start.4) | collective-permute-done | bytes 49184 | tf_op jit(solution)/shard_map/ppermute | solution.py:518
  43.7 0.0 collective-permute-done.5
  43.7 1.2 %shard_map.65 = (f32[3,4,8,128]{3,2,1,0:T(8,128)}, f32[3,4,8,128]{3,2,1,0:T(8,128)}) custom-call(f32[3,4,8,128]{3,2,1,0:T(8,128)S(1)} %get-tuple-element.37.near, f32[3,4,8,128]{3,2,1,0:T(8,128)S(1)} %get-tuple-element.38.v_in, f32[3,4,8,128]{3,2,1,0:T(8,128)S(1)} %get-tuple-element.40.force, f32[10,16,128]{2,1,0:T(8,128)S(1)} %get-tuple-element.41.s, ...), custom_call_target="tpu_custom_call" | custom-call | flops 1000 | bytes 1000 | tf_op jit(solution)/shard_map/pallas_call | solution.py:505
  (1 shorter events, 0.0 us)
Async XLA Ops:
  1.6 11.1 %collective-permute-start = (f32[20,8,128]{2,1,0:T(8,128)S(1)}, f32[20,8,128]{2,1,0:T(8,128)S(1)}, u32[]{:S(2)}, u32[]{:S(2)}) collective-permute-start(f32[20,8,128]{2,1,0:T(8,128)S(1)} %get-tuple-element.25), channel_id=1, source_target_pairs={{16,32},{48,64},{80,96},{112,128},{144,160},{176,192},{208,224},{2... | collective-permute-start | bytes 245768 | tf_op jit(solution)/shard_map/ppermute | solution.py:518
  7.9 6.3 %collective-permute-start.1 = (f32[20,8,128]{2,1,0:T(8,128)S(1)}, f32[20,8,128]{2,1,0:T(8,128)S(1)}, u32[]{:S(2)}, u32[]{:S(2)}) collective-permute-start(f32[20,8,128]{2,1,0:T(8,128)S(1)} %get-tuple-element.26), channel_id=1, source_target_pairs={{0,16},{32,48},{64,80},{96,112},{128,144},{160,176},{192,208},{224... | collective-permute-start | bytes 245768 | tf_op jit(solution)/shard_map/ppermute | solution.py:518
  9.8 0.8 %copy-start = (f32[3,4,8,128]{3,2,1,0:T(8,128)S(1)}, f32[3,4,8,128]{3,2,1,0:T(8,128)}, u32[]{:S(2)}) copy-start(f32[3,4,8,128]{3,2,1,0:T(8,128)} %v_in.1) | copy-start | bytes 147460
  14.8 18.6 %collective-permute-start.2 = (f32[176,128]{1,0:T(8,128)S(1)}, f32[176,128]{1,0:T(8,128)S(1)}, u32[]{:S(2)}, u32[]{:S(2)}) collective-permute-start(f32[176,128]{1,0:T(8,128)S(1)} %get-tuple-element.28), channel_id=1, source_target_pairs={{1,2},{3,4},{5,6},{7,8},{9,10},{11,12},{13,14},{2,1},{4,3},{6,5},{... | collective-permute-start | bytes 270344 | tf_op jit(solution)/shard_map/ppermute | solution.py:518
  17.1 16.3 %collective-permute-start.3 = (f32[176,128]{1,0:T(8,128)S(1)}, f32[176,128]{1,0:T(8,128)S(1)}, u32[]{:S(2)}, u32[]{:S(2)}) collective-permute-start(f32[176,128]{1,0:T(8,128)S(1)} %get-tuple-element.29), channel_id=1, source_target_pairs={{0,1},{2,3},{4,5},{6,7},{8,9},{10,11},{12,13},{14,15},{1,0},{3,2},... | collective-permute-start | bytes 270344 | tf_op jit(solution)/shard_map/ppermute | solution.py:518
  34.4 9.3 %collective-permute-start.4 = (f32[12,8,128]{2,1,0:T(8,128)S(1)}, f32[12,8,128]{2,1,0:T(8,128)S(1)}, u32[]{:S(2)}, u32[]{:S(2)}) collective-permute-start(f32[12,8,128]{2,1,0:T(8,128)S(1)} %bitcast.8), channel_id=1, source_target_pairs={{16,32},{48,64},{80,96},{112,128},{144,160},{176,192},{208,224},{2... | collective-permute-start | bytes 147464 | tf_op jit(solution)/shard_map/ppermute | solution.py:518
  37.7 6.0 %collective-permute-start.5 = (f32[12,8,128]{2,1,0:T(8,128)S(1)}, f32[12,8,128]{2,1,0:T(8,128)S(1)}, u32[]{:S(2)}, u32[]{:S(2)}) collective-permute-start(f32[12,8,128]{2,1,0:T(8,128)S(1)} %bitcast.7), channel_id=1, source_target_pairs={{0,16},{32,48},{64,80},{96,112},{128,144},{160,176},{192,208},{224... | collective-permute-start | bytes 147464 | tf_op jit(solution)/shard_map/ppermute | solution.py:518

commit v6 on v4

--- a/solution.py
+++ b/solution.py
@@ -123,7 +123,7 @@
     return [jnp.where(mask, rolled(p, -ez), 0.0) for p in part]
 
 
-def accumulate(plane, base, owned, reacted, u, ur, s, sr, d):
+def accumulate(plane, base, owned, reacted, u, ur, s, sr, d, turned):
     here = [u[(c,) + spot(u, plane, base)] for c in range(3)]
     total = [jnp.zeros((8, 128), jnp.float32) for _ in range(3)]
 
@@ -147,7 +147,12 @@
         bonds = [b for b in reacted if b[1][2] == ez]
         if not bonds:
             continue
-        moved = here if ez == 0 else [rolled(h, ez) for h in here]
+        if ez == 0:
+            moved = here
+        elif abs(ez) < 3:
+            moved = turned(ROLLS.index(ez))
+        else:
+            moved = [rolled(h, ez) for h in here]
         part = total if ez == 0 else [jnp.zeros((8, 128), jnp.float32) for _ in range(3)]
         for q, (ex, ey, _) in bonds:
             row, at = base - ey, plane - ex
@@ -294,7 +299,7 @@
 EACH = ((0,), (1,), (2,))
 
 
-def own_part(u, ur, s, sr, d, force):
+def own_part(u, ur, s, sr, d, force, kept):
     roll_field(u, ur, range(3, 7))
     roll_stiffness(s, sr, range(3, 7))
     for i in range(4):
@@ -302,20 +307,27 @@
             put_zeros(ur, [(c, i) for c in range(3)], (plane,), 0, ROWS)
             put_zeros(sr, [(i,)], (plane,), 0, ROWS)
 
+    for c in range(3):
+        for i in range(4):
+            for x in range(4):
+                kept[c, i, x] = ur[c, i, x + 3, LOW : LOW + 8]
+
     @pl.loop(0, 4)
     def _(x):
-        total = accumulate(x + 3, LOW, BONDS, BONDS, u, ur, s, sr, d)
+        turned = lambda i: [kept[c, i, x] for c in range(3)]
+        total = accumulate(x + 3, LOW, BONDS, BONDS, u, ur, s, sr, d, turned)
         for c in range(3):
             force[c, x] = total[c]
 
 
-def side_part(x, u, ur, s, sr, d):
+def side_part(x, u, ur, s, sr, d, kept):
     owned = [b for b in BONDS if x + b[1][0] > 3]
     reacted = [b for b in BONDS if x - b[1][0] < 0]
-    return accumulate(x + 3, LOW, owned, reacted, u, ur, s, sr, d)
-
-
-def first_own(fields, force, u, ur, s, sr, d):
+    turned = lambda i: [kept[c, i, x] for c in range(3)]
+    return accumulate(x + 3, LOW, owned, reacted, u, ur, s, sr, d, turned)
+
+
+def first_own(fields, force, kept, u, ur, s, sr, d):
     put_zeros(u, EACH, SIDES, 0, ROWS)
     put_zeros(s, [()], SIDES, 0, ROWS)
     for row, count in OUTER:
@@ -323,10 +335,10 @@
         put_zeros(s, [()], range(3, 7), row, count)
         put_zeros(d, [(w,) for w in range(6)], range(3, 7), row, count)
     put_own(fields, u, s, d)
-    own_part(u, ur, s, sr, d, force)
-
-
-def first_sides(fields, far_x, near_x, force, b, a, v_part, u, ur, s, sr, d, near, up, down):
+    own_part(u, ur, s, sr, d, force, kept)
+
+
+def first_sides(fields, far_x, near_x, force, kept, b, a, v_part, u, ur, s, sr, d, near, up, down):
     even_x, even = even_place()
     for row, count in OUTER:
         put_zeros(u, EACH, SIDES, row, count)
@@ -339,7 +351,7 @@
     roll_field(u, ur, (7, 8), (LOW,))
     roll_stiffness(s, sr, (7, 8), (LOW,))
     for x in range(4):
-        total = side_part(x, u, ur, s, sr, d)
+        total = side_part(x, u, ur, s, sr, d, kept)
         scale = bond_scale * s[spot(s, x + 3, LOW)]
         for c in range(3):
             velocity = fields[V + c, x] + time_step * (scale * (force[c, x] + total[c]))
@@ -434,7 +446,7 @@
             place += 2
 
 
-def last_own(fields, far_x, near_x, b, a, near, edge, force, s, sr, d, u, ur):
+def last_own(fields, far_x, near_x, b, a, near, edge, force, kept, s, sr, d, u, ur):
     even_x, even = even_place()
     put_zeros(u, EACH, SIDES, 0, ROWS)
     put_zeros(s, [()], SIDES, 0, ROWS)
@@ -445,13 +457,13 @@
         for row in (0, 1, 2, 11, 12, 13):
             for x in range(4):
                 u[c, x + 3, row : row + 1] = edge[c, line_of(row), x : x + 1]
-    own_part(u, ur, s, sr, d, force)
+    own_part(u, ur, s, sr, d, force, kept)
     put_sides(even_x, near_x, far_x, None, s, d)
     put_rows(even, a, b, s, d, SIDES)
     roll_stiffness(s, sr, (7, 8))
 
 
-def last_sides(near, v_in, force, s, sr, d, far_u, near_u, u_out, v_out, u, ur):
+def last_sides(near, v_in, force, kept, s, sr, d, far_u, near_u, u_out, v_out, u, ur):
     even_x, _ = even_place()
     for c in range(3):
         u[c, 3:7, LOW : LOW + 8] = near[c]
@@ -474,7 +486,7 @@
             place += 2
     roll_field(u, ur, (7, 8))
     for x in range(4):
-        total = side_part(x, u, ur, s, sr, d)
+        total = side_part(x, u, ur, s, sr, d, kept)
         scale = bond_scale * s[x + 3, LOW : LOW + 8]
         for c in range(3):
             velocity = v_in[c, x] + time_step * (scale * (force[c, x] + total[c]))
@@ -524,10 +536,11 @@
     far_x, near_x = call(pack_x, [f32(X_TILES, 8, 128)] * 2, [], fields)
     far_x = swapped(far_x, "gx", 1)
     near_x = swapped(near_x, "gx", 0)
-    (force,) = call(first_own, [point], LAYERS, fields, flops=4_000_000)
+    turned = f32(3, 4, 4, 8, 128)
+    force, kept = call(first_own, [point, turned], LAYERS, fields, flops=4_000_000)
     message = f32(Y_ROWS, 128)
     b, a, v_part = call(
-        first_sides, [message, message, point], FLAT + [FLAT[0], message, message], fields, far_x, near_x, force
+        first_sides, [message, message, point], FLAT + [FLAT[0], message, message], fields, far_x, near_x, force, kept
     )
     b = swapped(b, "gy", 1)
     a = swapped(a, "gy", 0)
@@ -545,7 +558,7 @@
     kept = (fields, far_x, near_x, b, a, near, edge)
     far_u = swapped(far_u.reshape(12, 8, 128), "gx", 1).reshape(96, 128)
     near_u = swapped(near_u.reshape(12, 8, 128), "gx", 0).reshape(96, 128)
-    force, *stiff = call(last_own, [point] + LAYERS[2:], LAYERS[:2], *kept, flops=4_000_000)
+    force, *stiff = call(last_own, [point, turned] + LAYERS[2:], LAYERS[:2], *kept, flops=4_000_000)
     return tuple(
         call(last_sides, [point, point], LAYERS[:2], near, velocity, force, *stiff, far_u, near_u)
     )

time: 44.9 us -> 44.8 us (level)
  Pallas kernels: 7.3 us -> 6.42 us
  waiting for transfers between devices: 16.5 us -> 17.2 us
    pallas_call x7, Pallas kernels: 7.3 us -> 6.42 us  [call(): pl.pallas_call(kernel, out_shape=outputs, in_specs=[pl.BlockSpec(memory_s...]
    ppermute x6, waiting for transfers between devices: 16.5 us -> 17.2 us  [swapped(): return lax.ppermute(value, axis, pairs + [(j, i) for i, j in pairs])]
  transfers between devices with their start and end apart: 6 -> 6, of which waited for: 4 -> 4; matrix products, arithmetic and copies ran while one was open for 0% -> 0% of each run, Pallas kernels for 10% -> 9%
where the time goes in v6:
time: 44.8 us; the launch traced here: 44.5 us
  starting transfers between devices  19.2 us (43%)
  waiting for transfers between devices  17.2 us (38%)
  Pallas kernels  6.42 us (14%)
  other arithmetic  0.91 us (2%)
  between operations  0.73 us (2%)
    ppermute x6, starting transfers between devices, swapped(): return lax.ppermute(value, axis, pairs + [(j, i) for i, j in pairs])  19.2 us
    ppermute x6, waiting for transfers between devices, swapped(): return lax.ppermute(value, axis, pairs + [(j, i) for i, j in pairs])  17.2 us
    pallas_call x7, Pallas kernels, call(): pl.pallas_call(kernel, out_shape=outputs, in_specs=[pl.BlockSpec(memory_s...  6.42 us
    add x1, other arithmetic, joined_fields(): total + lax.pad(part, part.dtype.type(0), widths).astype(jnp.float32)  0.91 us
  transfers between devices with their start and end apart: 6, of which 4 were waited for; matrix products, arithmetic and copies ran while one was open for 0% of the time, Pallas kernels for 9%

profile of v6, /device:TPU:384, one launch (start us, length us, event | category | flops | bytes accessed | tf_op | source)
XLA Modules:
  0.0 44.5 jit_solution(17749359493036055189)
XLA Ops:
  0.6 0.9 %convert_add_fusion.fields = f32[13,4,8,128]{3,2,1,0:T(8,128)S(1)} fusion(s32[6,4,8,128]{3,2,1,0:T(8,128)} %param.7, f32[1,4,8,128]{3,2,1,0:T(8,128)} %bitcast.9, f32[3,4,8,128]{3,2,1,0:T(8,128)} %param.5, f32[3,4,8,128]{3,2,1,0:T(8,128)} %param.4), kind=kLoop, calls=%fused_computation | loop fusion | flops 212992 | bytes 425984 | tf_op jit(solution)/shard_map/add | solution.py:277
  1.6 6.3 %collective-permute-start = (f32[20,8,128]{2,1,0:T(8,128)S(1)}, f32[20,8,128]{2,1,0:T(8,128)S(1)}, u32[]{:S(2)}, u32[]{:S(2)}) collective-permute-start(f32[20,8,128]{2,1,0:T(8,128)S(1)} %get-tuple-element.25), channel_id=1, source_target_pairs={{16,32},{48,64},{80,96},{112,128},{144,160},{176,192},{208,224},{2... | collective-permute-start | bytes 245768 | tf_op jit(solution)/shard_map/ppermute | solution.py:529
  7.9 1.9 %collective-permute-start.1 = (f32[20,8,128]{2,1,0:T(8,128)S(1)}, f32[20,8,128]{2,1,0:T(8,128)S(1)}, u32[]{:S(2)}, u32[]{:S(2)}) collective-permute-start(f32[20,8,128]{2,1,0:T(8,128)S(1)} %get-tuple-element.26), channel_id=1, source_target_pairs={{0,16},{32,48},{64,80},{96,112},{128,144},{160,176},{192,208},{224... | collective-permute-start | bytes 245768 | tf_op jit(solution)/shard_map/ppermute | solution.py:529
  9.8 1.7 %shard_map.60 = (f32[3,4,8,128]{3,2,1,0:T(8,128)S(1)}, f32[3,4,4,8,128]{4,3,2,1,0:T(8,128)S(1)}) custom-call(f32[13,4,8,128]{3,2,1,0:T(8,128)S(1)} %convert_add_fusion.fields), custom_call_target="tpu_custom_call" | custom-call | flops 4000000 | bytes 4000000 | tf_op jit(solution)/shard_map/pallas_call | solution.py:516
  11.5 0.0 collective-permute-done.far_x
  11.5 2.7 %collective-permute-done.1.near_x = f32[20,8,128]{2,1,0:T(8,128)S(1)} collective-permute-done((f32[20,8,128]{2,1,0:T(8,128)S(1)}, f32[20,8,128]{2,1,0:T(8,128)S(1)}, u32[]{:S(2)}, u32[]{:S(2)}) %collective-permute-start.1) | collective-permute-done | bytes 81952 | tf_op jit(solution)/shard_map/ppermute | solution.py:529
  14.2 0.5 %shard_map.61 = (f32[176,128]{1,0:T(8,128)S(1)}, f32[176,128]{1,0:T(8,128)S(1)}, f32[3,4,8,128]{3,2,1,0:T(8,128)S(1)}) custom-call(f32[13,4,8,128]{3,2,1,0:T(8,128)S(1)} %convert_add_fusion.fields, f32[20,8,128]{2,1,0:T(8,128)S(1)} %collective-permute-done.far_x, f32[20,8,128]{2,1,0:T(8,128)S(1)} %collective-permute-done.1.near_x, ...), custom_call_target="tpu_custom_call" | custom-call | flops 1000 | bytes 1000 | tf_op jit(solution)/shard_map/pallas_call | solution.py:516
  14.8 2.3 %collective-permute-start.2 = (f32[176,128]{1,0:T(8,128)S(1)}, f32[176,128]{1,0:T(8,128)S(1)}, u32[]{:S(2)}, u32[]{:S(2)}) collective-permute-start(f32[176,128]{1,0:T(8,128)S(1)} %get-tuple-element.29), channel_id=1, source_target_pairs={{1,2},{3,4},{5,6},{7,8},{9,10},{11,12},{13,14},{2,1},{4,3},{6,5},{... | collective-permute-start | bytes 270344 | tf_op jit(solution)/shard_map/ppermute | solution.py:529
  17.1 3.2 %collective-permute-start.3 = (f32[176,128]{1,0:T(8,128)S(1)}, f32[176,128]{1,0:T(8,128)S(1)}, u32[]{:S(2)}, u32[]{:S(2)}) collective-permute-start(f32[176,128]{1,0:T(8,128)S(1)} %get-tuple-element.30), channel_id=1, source_target_pairs={{0,1},{2,3},{4,5},{6,7},{8,9},{10,11},{12,13},{14,15},{1,0},{3,2},... | collective-permute-start | bytes 270344 | tf_op jit(solution)/shard_map/ppermute | solution.py:529
  20.3 0.4 shard_map.62
  20.7 12.3 %collective-permute-done.2.b = f32[176,128]{1,0:T(8,128)S(1)} collective-permute-done((f32[176,128]{1,0:T(8,128)S(1)}, f32[176,128]{1,0:T(8,128)S(1)}, u32[]{:S(2)}, u32[]{:S(2)}) %collective-permute-start.2) | collective-permute-done | bytes 90144 | tf_op jit(solution)/shard_map/ppermute | solution.py:529
  32.9 0.0 collective-permute-done.3.a
  32.9 0.9 %shard_map.63 = (f32[3,4,8,128]{3,2,1,0:T(8,128)S(1)}, f32[3,4,8,128]{3,2,1,0:T(8,128)S(1)}, f32[3,6,8,128]{3,2,1,0:T(8,128)S(1)}, f32[96,128]{1,0:T(8,128)S(1)}, f32[96,128]{1,0:T(8,128)S(1)}) custom-call(f32[13,4,8,128]{3,2,1,0:T(8,128)S(1)} %convert_add_fusion.fields, f32[176,128]{1,0:T(8,128)S(1)} %collective-permute-done.2.b, ...), custom_call_target="tpu_custom_call" | custom-call | flops 1000 | bytes 1000 | tf_op jit(solution)/shard_map/pallas_call | solution.py:516
  33.9 3.5 %collective-permute-start.4 = (f32[12,8,128]{2,1,0:T(8,128)S(1)}, f32[12,8,128]{2,1,0:T(8,128)S(1)}, u32[]{:S(2)}, u32[]{:S(2)}) collective-permute-start(f32[12,8,128]{2,1,0:T(8,128)S(1)} %bitcast.8), channel_id=1, source_target_pairs={{16,32},{48,64},{80,96},{112,128},{144,160},{176,192},{208,224},{2... | collective-permute-start | bytes 147464 | tf_op jit(solution)/shard_map/ppermute | solution.py:529
  37.4 1.9 %collective-permute-start.5 = (f32[12,8,128]{2,1,0:T(8,128)S(1)}, f32[12,8,128]{2,1,0:T(8,128)S(1)}, u32[]{:S(2)}, u32[]{:S(2)}) collective-permute-start(f32[12,8,128]{2,1,0:T(8,128)S(1)} %bitcast.7), channel_id=1, source_target_pairs={{0,16},{32,48},{64,80},{96,112},{128,144},{160,176},{192,208},{224... | collective-permute-start | bytes 147464 | tf_op jit(solution)/shard_map/ppermute | solution.py:529
  39.4 1.8 %shard_map.64 = (f32[3,4,8,128]{3,2,1,0:T(8,128)S(1)}, f32[3,4,4,8,128]{4,3,2,1,0:T(8,128)S(1)}, f32[10,16,128]{2,1,0:T(8,128)S(1)}, f32[4,10,16,128]{3,2,1,0:T(8,128)S(1)}, s32[6,10,16,128]{3,2,1,0:T(8,128)S(1)}) custom-call(f32[13,4,8,128]{3,2,1,0:T(8,128)S(1)} %convert_add_fusion.fields, f32[20,8,128]{2,1,0:T(8,128)S(1)} %collective-permute-done.far_x, ...), custom_call_target="tpu_custom_call" | custom-call | flops 4000000 | bytes 4000000 | tf_op jit(solution)/shard_map/pallas_call | solution.py:516
  41.2 2.0 %collective-permute-done.4 = f32[12,8,128]{2,1,0:T(8,128)S(1)} collective-permute-done((f32[12,8,128]{2,1,0:T(8,128)S(1)}, f32[12,8,128]{2,1,0:T(8,128)S(1)}, u32[]{:S(2)}, u32[]{:S(2)}) %collective-permute-start.4) | collective-permute-done | bytes 49184 | tf_op jit(solution)/shard_map/ppermute | solution.py:529
  43.2 0.2 collective-permute-done.5
  43.4 1.1 %shard_map.65 = (f32[3,4,8,128]{3,2,1,0:T(8,128)}, f32[3,4,8,128]{3,2,1,0:T(8,128)}) custom-call(f32[3,4,8,128]{3,2,1,0:T(8,128)S(1)} %get-tuple-element.38.near, f32[3,4,8,128]{3,2,1,0:T(8,128)S(1)} %get-tuple-element.39.v_in, f32[3,4,8,128]{3,2,1,0:T(8,128)S(1)} %get-tuple-element.41.force, f32[3,4,4,8,128]{4,3,2,1,0:T(8,128)S(1)} %get-tuple-element.42.kept, ...), custom_call_target="tpu_custom_call" | custom-call | flops 1000 | bytes 1000 | tf_op jit(solution)/shard_map/pallas_call | solution.py:516
  (1 shorter events, 0.0 us)
Async XLA Ops:
  1.6 10.0 %collective-permute-start = (f32[20,8,128]{2,1,0:T(8,128)S(1)}, f32[20,8,128]{2,1,0:T(8,128)S(1)}, u32[]{:S(2)}, u32[]{:S(2)}) collective-permute-start(f32[20,8,128]{2,1,0:T(8,128)S(1)} %get-tuple-element.25), channel_id=1, source_target_pairs={{16,32},{48,64},{80,96},{112,128},{144,160},{176,192},{208,224},{2... | collective-permute-start | bytes 245768 | tf_op jit(solution)/shard_map/ppermute | solution.py:529
  7.9 6.3 %collective-permute-start.1 = (f32[20,8,128]{2,1,0:T(8,128)S(1)}, f32[20,8,128]{2,1,0:T(8,128)S(1)}, u32[]{:S(2)}, u32[]{:S(2)}) collective-permute-start(f32[20,8,128]{2,1,0:T(8,128)S(1)} %get-tuple-element.26), channel_id=1, source_target_pairs={{0,16},{32,48},{64,80},{96,112},{128,144},{160,176},{192,208},{224... | collective-permute-start | bytes 245768 | tf_op jit(solution)/shard_map/ppermute | solution.py:529
  14.8 18.1 %collective-permute-start.2 = (f32[176,128]{1,0:T(8,128)S(1)}, f32[176,128]{1,0:T(8,128)S(1)}, u32[]{:S(2)}, u32[]{:S(2)}) collective-permute-start(f32[176,128]{1,0:T(8,128)S(1)} %get-tuple-element.29), channel_id=1, source_target_pairs={{1,2},{3,4},{5,6},{7,8},{9,10},{11,12},{13,14},{2,1},{4,3},{6,5},{... | collective-permute-start | bytes 270344 | tf_op jit(solution)/shard_map/ppermute | solution.py:529
  17.1 15.9 %collective-permute-start.3 = (f32[176,128]{1,0:T(8,128)S(1)}, f32[176,128]{1,0:T(8,128)S(1)}, u32[]{:S(2)}, u32[]{:S(2)}) collective-permute-start(f32[176,128]{1,0:T(8,128)S(1)} %get-tuple-element.30), channel_id=1, source_target_pairs={{0,1},{2,3},{4,5},{6,7},{8,9},{10,11},{12,13},{14,15},{1,0},{3,2},... | collective-permute-start | bytes 270344 | tf_op jit(solution)/shard_map/ppermute | solution.py:529
  33.9 9.3 %collective-permute-start.4 = (f32[12,8,128]{2,1,0:T(8,128)S(1)}, f32[12,8,128]{2,1,0:T(8,128)S(1)}, u32[]{:S(2)}, u32[]{:S(2)}) collective-permute-start(f32[12,8,128]{2,1,0:T(8,128)S(1)} %bitcast.8), channel_id=1, source_target_pairs={{16,32},{48,64},{80,96},{112,128},{144,160},{176,192},{208,224},{2... | collective-permute-start | bytes 147464 | tf_op jit(solution)/shard_map/ppermute | solution.py:529
  37.4 6.0 %collective-permute-start.5 = (f32[12,8,128]{2,1,0:T(8,128)S(1)}, f32[12,8,128]{2,1,0:T(8,128)S(1)}, u32[]{:S(2)}, u32[]{:S(2)}) collective-permute-start(f32[12,8,128]{2,1,0:T(8,128)S(1)} %bitcast.7), channel_id=1, source_target_pairs={{0,16},{32,48},{64,80},{96,112},{128,144},{160,176},{192,208},{224... | collective-permute-start | bytes 147464 | tf_op jit(solution)/shard_map/ppermute | solution.py:529

commit v7 on v6

--- a/solution.py
+++ b/solution.py
@@ -141,7 +141,7 @@
             else:
                 source = [rolled(h, ez) for h in here]
                 stiff = jnp.where(lane_mask(ez), rolled(s[spot(s, at, row)], ez), 0.0)
-            target = [h - float(e) for h, e in zip(here, (ex, ey, ez))]
+            target = [h - float(e) if e else h for h, e in zip(here, (ex, ey, ez))]
             words = d[(q // 11,) + spot(d, plane, base)]
             total = add_bond(total, source, target, length, intact(q, words, stiff))
         bonds = [b for b in reacted if b[1][2] == ez]
@@ -158,7 +158,7 @@
             row, at = base - ey, plane - ex
             length = math.sqrt(ex * ex + ey * ey + ez * ez)
             source = [u[(c,) + spot(u, at, row)] for c in range(3)]
-            target = [h + float(e) for h, e in zip(moved, (ex, ey, ez))]
+            target = [h + float(e) if e else h for h, e in zip(moved, (ex, ey, ez))]
             stiff = s[spot(s, at, row)]
             words = d[(q // 11,) + spot(d, at, row)]
             part = add_bond(part, source, target, length, intact(q, words, stiff))
@@ -191,7 +191,7 @@
                 word = d[q // 11, line_of(row), 2:10]
             else:
                 word = line(od, odr, (q // 11,), ez, plane, at)
-            target = [h - float(e) for h, e in zip(here, (ex, ey, ez))]
+            target = [h - float(e) if e else h for h, e in zip(here, (ex, ey, ez))]
             total = add_bond(total, source, target, length, intact(q, word, stiff))
     return [part[0:4] for part in total]
 

time: 44.8 us -> 44.8 us (level)
  no operation moved by 1% of the time
where the time goes in v7:
time: 44.8 us; the launch traced here: 44.5 us
  starting transfers between devices  19.2 us (43%)
  waiting for transfers between devices  17.2 us (38%)
  Pallas kernels  6.42 us (14%)
  other arithmetic  0.91 us (2%)
  between operations  0.73 us (2%)
    ppermute x6, starting transfers between devices, swapped(): return lax.ppermute(value, axis, pairs + [(j, i) for i, j in pairs])  19.2 us
    ppermute x6, waiting for transfers between devices, swapped(): return lax.ppermute(value, axis, pairs + [(j, i) for i, j in pairs])  17.2 us
    pallas_call x7, Pallas kernels, call(): pl.pallas_call(kernel, out_shape=outputs, in_specs=[pl.BlockSpec(memory_s...  6.42 us
    add x1, other arithmetic, joined_fields(): total + lax.pad(part, part.dtype.type(0), widths).astype(jnp.float32)  0.91 us
  transfers between devices with their start and end apart: 6, of which 4 were waited for; matrix products, arithmetic and copies ran while one was open for 0% of the time, Pallas kernels for 9%

profile of v7, /device:TPU:384, one launch (start us, length us, event | category | flops | bytes accessed | tf_op | source)
XLA Modules:
  0.0 44.5 jit_solution(17749359493036055189)
XLA Ops:
  0.6 0.9 %convert_add_fusion.fields = f32[13,4,8,128]{3,2,1,0:T(8,128)S(1)} fusion(s32[6,4,8,128]{3,2,1,0:T(8,128)} %param.7, f32[1,4,8,128]{3,2,1,0:T(8,128)} %bitcast.9, f32[3,4,8,128]{3,2,1,0:T(8,128)} %param.5, f32[3,4,8,128]{3,2,1,0:T(8,128)} %param.4), kind=kLoop, calls=%fused_computation | loop fusion | flops 212992 | bytes 425984 | tf_op jit(solution)/shard_map/add | solution.py:277
  1.6 6.3 %collective-permute-start = (f32[20,8,128]{2,1,0:T(8,128)S(1)}, f32[20,8,128]{2,1,0:T(8,128)S(1)}, u32[]{:S(2)}, u32[]{:S(2)}) collective-permute-start(f32[20,8,128]{2,1,0:T(8,128)S(1)} %get-tuple-element.25), channel_id=1, source_target_pairs={{16,32},{48,64},{80,96},{112,128},{144,160},{176,192},{208,224},{2... | collective-permute-start | bytes 245768 | tf_op jit(solution)/shard_map/ppermute | solution.py:529
  7.9 1.9 %collective-permute-start.1 = (f32[20,8,128]{2,1,0:T(8,128)S(1)}, f32[20,8,128]{2,1,0:T(8,128)S(1)}, u32[]{:S(2)}, u32[]{:S(2)}) collective-permute-start(f32[20,8,128]{2,1,0:T(8,128)S(1)} %get-tuple-element.26), channel_id=1, source_target_pairs={{0,16},{32,48},{64,80},{96,112},{128,144},{160,176},{192,208},{224... | collective-permute-start | bytes 245768 | tf_op jit(solution)/shard_map/ppermute | solution.py:529
  9.8 1.7 %shard_map.60 = (f32[3,4,8,128]{3,2,1,0:T(8,128)S(1)}, f32[3,4,4,8,128]{4,3,2,1,0:T(8,128)S(1)}) custom-call(f32[13,4,8,128]{3,2,1,0:T(8,128)S(1)} %convert_add_fusion.fields), custom_call_target="tpu_custom_call" | custom-call | flops 4000000 | bytes 4000000 | tf_op jit(solution)/shard_map/pallas_call | solution.py:516
  11.5 0.0 collective-permute-done.far_x
  11.5 2.7 %collective-permute-done.1.near_x = f32[20,8,128]{2,1,0:T(8,128)S(1)} collective-permute-done((f32[20,8,128]{2,1,0:T(8,128)S(1)}, f32[20,8,128]{2,1,0:T(8,128)S(1)}, u32[]{:S(2)}, u32[]{:S(2)}) %collective-permute-start.1) | collective-permute-done | bytes 81952 | tf_op jit(solution)/shard_map/ppermute | solution.py:529
  14.2 0.5 %shard_map.61 = (f32[176,128]{1,0:T(8,128)S(1)}, f32[176,128]{1,0:T(8,128)S(1)}, f32[3,4,8,128]{3,2,1,0:T(8,128)S(1)}) custom-call(f32[13,4,8,128]{3,2,1,0:T(8,128)S(1)} %convert_add_fusion.fields, f32[20,8,128]{2,1,0:T(8,128)S(1)} %collective-permute-done.far_x, f32[20,8,128]{2,1,0:T(8,128)S(1)} %collective-permute-done.1.near_x, ...), custom_call_target="tpu_custom_call" | custom-call | flops 1000 | bytes 1000 | tf_op jit(solution)/shard_map/pallas_call | solution.py:516
  14.8 2.3 %collective-permute-start.2 = (f32[176,128]{1,0:T(8,128)S(1)}, f32[176,128]{1,0:T(8,128)S(1)}, u32[]{:S(2)}, u32[]{:S(2)}) collective-permute-start(f32[176,128]{1,0:T(8,128)S(1)} %get-tuple-element.29), channel_id=1, source_target_pairs={{1,2},{3,4},{5,6},{7,8},{9,10},{11,12},{13,14},{2,1},{4,3},{6,5},{... | collective-permute-start | bytes 270344 | tf_op jit(solution)/shard_map/ppermute | solution.py:529
  17.1 3.2 %collective-permute-start.3 = (f32[176,128]{1,0:T(8,128)S(1)}, f32[176,128]{1,0:T(8,128)S(1)}, u32[]{:S(2)}, u32[]{:S(2)}) collective-permute-start(f32[176,128]{1,0:T(8,128)S(1)} %get-tuple-element.30), channel_id=1, source_target_pairs={{0,1},{2,3},{4,5},{6,7},{8,9},{10,11},{12,13},{14,15},{1,0},{3,2},... | collective-permute-start | bytes 270344 | tf_op jit(solution)/shard_map/ppermute | solution.py:529
  20.3 0.4 shard_map.62
  20.7 12.3 %collective-permute-done.2.b = f32[176,128]{1,0:T(8,128)S(1)} collective-permute-done((f32[176,128]{1,0:T(8,128)S(1)}, f32[176,128]{1,0:T(8,128)S(1)}, u32[]{:S(2)}, u32[]{:S(2)}) %collective-permute-start.2) | collective-permute-done | bytes 90144 | tf_op jit(solution)/shard_map/ppermute | solution.py:529
  32.9 0.0 collective-permute-done.3.a
  32.9 0.9 %shard_map.63 = (f32[3,4,8,128]{3,2,1,0:T(8,128)S(1)}, f32[3,4,8,128]{3,2,1,0:T(8,128)S(1)}, f32[3,6,8,128]{3,2,1,0:T(8,128)S(1)}, f32[96,128]{1,0:T(8,128)S(1)}, f32[96,128]{1,0:T(8,128)S(1)}) custom-call(f32[13,4,8,128]{3,2,1,0:T(8,128)S(1)} %convert_add_fusion.fields, f32[176,128]{1,0:T(8,128)S(1)} %collective-permute-done.2.b, ...), custom_call_target="tpu_custom_call" | custom-call | flops 1000 | bytes 1000 | tf_op jit(solution)/shard_map/pallas_call | solution.py:516
  33.9 3.5 %collective-permute-start.4 = (f32[12,8,128]{2,1,0:T(8,128)S(1)}, f32[12,8,128]{2,1,0:T(8,128)S(1)}, u32[]{:S(2)}, u32[]{:S(2)}) collective-permute-start(f32[12,8,128]{2,1,0:T(8,128)S(1)} %bitcast.8), channel_id=1, source_target_pairs={{16,32},{48,64},{80,96},{112,128},{144,160},{176,192},{208,224},{2... | collective-permute-start | bytes 147464 | tf_op jit(solution)/shard_map/ppermute | solution.py:529
  37.4 1.9 %collective-permute-start.5 = (f32[12,8,128]{2,1,0:T(8,128)S(1)}, f32[12,8,128]{2,1,0:T(8,128)S(1)}, u32[]{:S(2)}, u32[]{:S(2)}) collective-permute-start(f32[12,8,128]{2,1,0:T(8,128)S(1)} %bitcast.7), channel_id=1, source_target_pairs={{0,16},{32,48},{64,80},{96,112},{128,144},{160,176},{192,208},{224... | collective-permute-start | bytes 147464 | tf_op jit(solution)/shard_map/ppermute | solution.py:529
  39.4 1.8 %shard_map.64 = (f32[3,4,8,128]{3,2,1,0:T(8,128)S(1)}, f32[3,4,4,8,128]{4,3,2,1,0:T(8,128)S(1)}, f32[10,16,128]{2,1,0:T(8,128)S(1)}, f32[4,10,16,128]{3,2,1,0:T(8,128)S(1)}, s32[6,10,16,128]{3,2,1,0:T(8,128)S(1)}) custom-call(f32[13,4,8,128]{3,2,1,0:T(8,128)S(1)} %convert_add_fusion.fields, f32[20,8,128]{2,1,0:T(8,128)S(1)} %collective-permute-done.far_x, ...), custom_call_target="tpu_custom_call" | custom-call | flops 4000000 | bytes 4000000 | tf_op jit(solution)/shard_map/pallas_call | solution.py:516
  41.2 2.0 %collective-permute-done.4 = f32[12,8,128]{2,1,0:T(8,128)S(1)} collective-permute-done((f32[12,8,128]{2,1,0:T(8,128)S(1)}, f32[12,8,128]{2,1,0:T(8,128)S(1)}, u32[]{:S(2)}, u32[]{:S(2)}) %collective-permute-start.4) | collective-permute-done | bytes 49184 | tf_op jit(solution)/shard_map/ppermute | solution.py:529
  43.2 0.2 collective-permute-done.5
  43.4 1.1 %shard_map.65 = (f32[3,4,8,128]{3,2,1,0:T(8,128)}, f32[3,4,8,128]{3,2,1,0:T(8,128)}) custom-call(f32[3,4,8,128]{3,2,1,0:T(8,128)S(1)} %get-tuple-element.38.near, f32[3,4,8,128]{3,2,1,0:T(8,128)S(1)} %get-tuple-element.39.v_in, f32[3,4,8,128]{3,2,1,0:T(8,128)S(1)} %get-tuple-element.41.force, f32[3,4,4,8,128]{4,3,2,1,0:T(8,128)S(1)} %get-tuple-element.42.kept, ...), custom_call_target="tpu_custom_call" | custom-call | flops 1000 | bytes 1000 | tf_op jit(solution)/shard_map/pallas_call | solution.py:516
  (1 shorter events, 0.0 us)
Async XLA Ops:
  1.6 10.0 %collective-permute-start = (f32[20,8,128]{2,1,0:T(8,128)S(1)}, f32[20,8,128]{2,1,0:T(8,128)S(1)}, u32[]{:S(2)}, u32[]{:S(2)}) collective-permute-start(f32[20,8,128]{2,1,0:T(8,128)S(1)} %get-tuple-element.25), channel_id=1, source_target_pairs={{16,32},{48,64},{80,96},{112,128},{144,160},{176,192},{208,224},{2... | collective-permute-start | bytes 245768 | tf_op jit(solution)/shard_map/ppermute | solution.py:529
  7.9 6.3 %collective-permute-start.1 = (f32[20,8,128]{2,1,0:T(8,128)S(1)}, f32[20,8,128]{2,1,0:T(8,128)S(1)}, u32[]{:S(2)}, u32[]{:S(2)}) collective-permute-start(f32[20,8,128]{2,1,0:T(8,128)S(1)} %get-tuple-element.26), channel_id=1, source_target_pairs={{0,16},{32,48},{64,80},{96,112},{128,144},{160,176},{192,208},{224... | collective-permute-start | bytes 245768 | tf_op jit(solution)/shard_map/ppermute | solution.py:529
  14.8 18.1 %collective-permute-start.2 = (f32[176,128]{1,0:T(8,128)S(1)}, f32[176,128]{1,0:T(8,128)S(1)}, u32[]{:S(2)}, u32[]{:S(2)}) collective-permute-start(f32[176,128]{1,0:T(8,128)S(1)} %get-tuple-element.29), channel_id=1, source_target_pairs={{1,2},{3,4},{5,6},{7,8},{9,10},{11,12},{13,14},{2,1},{4,3},{6,5},{... | collective-permute-start | bytes 270344 | tf_op jit(solution)/shard_map/ppermute | solution.py:529
  17.1 15.9 %collective-permute-start.3 = (f32[176,128]{1,0:T(8,128)S(1)}, f32[176,128]{1,0:T(8,128)S(1)}, u32[]{:S(2)}, u32[]{:S(2)}) collective-permute-start(f32[176,128]{1,0:T(8,128)S(1)} %get-tuple-element.30), channel_id=1, source_target_pairs={{0,1},{2,3},{4,5},{6,7},{8,9},{10,11},{12,13},{14,15},{1,0},{3,2},... | collective-permute-start | bytes 270344 | tf_op jit(solution)/shard_map/ppermute | solution.py:529
  33.9 9.3 %collective-permute-start.4 = (f32[12,8,128]{2,1,0:T(8,128)S(1)}, f32[12,8,128]{2,1,0:T(8,128)S(1)}, u32[]{:S(2)}, u32[]{:S(2)}) collective-permute-start(f32[12,8,128]{2,1,0:T(8,128)S(1)} %bitcast.8), channel_id=1, source_target_pairs={{16,32},{48,64},{80,96},{112,128},{144,160},{176,192},{208,224},{2... | collective-permute-start | bytes 147464 | tf_op jit(solution)/shard_map/ppermute | solution.py:529
  37.4 6.0 %collective-permute-start.5 = (f32[12,8,128]{2,1,0:T(8,128)S(1)}, f32[12,8,128]{2,1,0:T(8,128)S(1)}, u32[]{:S(2)}, u32[]{:S(2)}) collective-permute-start(f32[12,8,128]{2,1,0:T(8,128)S(1)} %bitcast.7), channel_id=1, source_target_pairs={{0,16},{32,48},{64,80},{96,112},{128,144},{160,176},{192,208},{224... | collective-permute-start | bytes 147464 | tf_op jit(solution)/shard_map/ppermute | solution.py:529
